TPU v7x, 32 devices: a whole 2x2x4 slice. The times are simulated.
32 devices in a mesh: dp: 8 (over z, y), tp: 4 (over x, core).
Axes of the slice: x: 2, y: 2, z: 4, core: 2. Of those that a mesh axis runs over, the one named last changes fastest.
Arguments:
- prefill_latent: bfloat16 [1024, 576], P('dp'), may hold values from -5 to 5
- request_slot: int32 [32], replicated, may hold values from 0 to 31, each once
- new_lengths: int32 [8, 4], replicated, may hold values from 1 to 8, 16 in all within a row
- ctx_lengths: int32 [32], P('dp'), may hold values from 1 to 1024, 16384 in all
- kv_cache: bfloat16 [32, 1024, 576], P('dp'), may hold values from -5 to 5
- queries: bfloat16 [2, 32, 128, 576], P(None, 'dp', 'tp'), may hold values from -48 to 48
- step_latents: bfloat16 [2, 32, 576], P(None, 'dp'), may hold values from -5 to 5
- w_uv: bfloat16 [128, 512, 128], P('tp'), may hold values from -0.25 to 0.25
- w_out: bfloat16 [128, 128, 7168], P('tp', None, 'dp'), may hold values from -0.0625 to 0.0625
- hidden: bfloat16 [2, 32, 7168], P(None, None, ('dp', 'tp')), may hold values from -2 to 2
- ffn_gain: float32 [7168], replicated, may hold values from 0.5 to 1.5
- w_gate: bfloat16 [7168, 18432], P(None, ('dp', 'tp')), may hold values from -0.0625 to 0.0625
- w_up: bfloat16 [7168, 18432], P(None, ('dp', 'tp')), may hold values from -0.0625 to 0.0625
- w_down: bfloat16 [18432, 7168], P(('dp', 'tp')), may hold values from -0.078125 to 0.078125
Outputs:
- layer_out: bfloat16 [2, 32, 7168], P(None, None, ('dp', 'tp'))
Inputs may be any that keep to these rules, and one draw needn't show every extreme that they name: A permutation of the 32 requests; the owner of request r is request_slot[r] // 4. `new_lengths`: row j lists the 4 requests of owner j; each row sums to 16, and its largest entry is 8. `ctx_lengths`: sums to 16384; the largest is 1024.
All inputs are finite; a program needn't handle non-finite values. No bound on the sum of `ctx_lengths` on one device may be relied on, other than what follows from the above.
Results may differ from a plain program's by a relative error of at most 0.02.
Values may be sent and summed in bfloat16 or wider, within the bound.
A program may use at most 128 MiB of HBM per device.

v0:
```python
import jax
import jax.numpy as jnp
from jax import lax
from jax.sharding import PartitionSpec as P

LAT = 512
QKD = 192
OWN_TOK = 16


masked_score = -1e30
norm_eps = 1e-06


def attend(query, step_ids, kv_cache, cache_mask, new_rows, new_mask, step_latents, w_uv):
    score_scale = QKD ** (-0.5)
    cache_scores = (
        jnp.einsum("sqhc,qkc->sqhk", query, kv_cache, preferred_element_type=jnp.float32)
        * score_scale
    )
    cache_scores = jnp.where(cache_mask[None, :, None, :], cache_scores, masked_score)
    fresh_scores = (
        jnp.einsum("sqhc,kc->sqhk", query, new_rows, preferred_element_type=jnp.float32)
        * score_scale
    )
    fresh_scores = jnp.where(new_mask[None, :, None, :], fresh_scores, masked_score)
    token_scores = (
        jnp.einsum("sqhc,tqc->sqht", query, step_latents, preferred_element_type=jnp.float32)
        * score_scale
    )
    token_valid = jnp.arange(step_latents.shape[0], dtype=jnp.int32)[None, :] <= step_ids[:, None]
    token_scores = jnp.where(token_valid[:, None, None, :], token_scores, masked_score)
    highest = jnp.maximum(
        jnp.maximum(jnp.max(cache_scores, axis=-1), jnp.max(fresh_scores, axis=-1)),
        jnp.max(token_scores, axis=-1),
    )[..., None]
    cache_exp = jnp.exp(cache_scores - highest)
    fresh_exp = jnp.exp(fresh_scores - highest)
    token_exp = jnp.exp(token_scores - highest)
    totals = (
        jnp.sum(cache_exp, axis=-1, keepdims=True)
        + jnp.sum(fresh_exp, axis=-1, keepdims=True)
        + jnp.sum(token_exp, axis=-1, keepdims=True)
    )
    cache_probs = (cache_exp / totals).astype(jnp.bfloat16)
    fresh_probs = (fresh_exp / totals).astype(jnp.bfloat16)
    token_probs = (token_exp / totals).astype(jnp.bfloat16)
    latent_out = jnp.einsum(
        "sqhk,qkc->sqhc", cache_probs, kv_cache[:, :, :LAT], preferred_element_type=jnp.float32
    )
    latent_out = latent_out + jnp.einsum(
        "sqhk,kc->sqhc", fresh_probs, new_rows[:, :LAT], preferred_element_type=jnp.float32
    )
    latent_out = latent_out + jnp.einsum(
        "sqht,tqc->sqhc", token_probs, step_latents[:, :, :LAT], preferred_element_type=jnp.float32
    )
    latent_out = latent_out.astype(jnp.bfloat16)
    return jnp.einsum(
        "sqhc,hcv->sqhv", latent_out, w_uv, preferred_element_type=jnp.float32
    ).astype(jnp.bfloat16)


def shards(
    prefill_latent,
    request_slot,
    new_lengths,
    ctx_lengths,
    kv_cache,
    queries,
    step_latents,
    w_uv,
    w_out,
    hidden,
    ffn_gain,
    w_gate,
    w_up,
    w_down,
):
    dp_count = lax.axis_size("dp")
    dp_rank = lax.axis_index("dp")
    tp_rank = lax.axis_index("tp")
    per_owner = new_lengths.shape[1]
    total_requests = request_slot.shape[0]
    latent_width = kv_cache.shape[2]
    share_width = hidden.shape[2]
    block_width = w_out.shape[2]
    model_width = block_width * dp_count
    numbers = jnp.arange(total_requests, dtype=jnp.int32)
    one_hot = request_slot[:, None] == numbers[None, :]
    lengths_flat = new_lengths.reshape(-1)
    request_rows = jnp.sum(jnp.where(one_hot, lengths_flat[None, :], 0), axis=1)
    offsets = jnp.cumsum(request_rows) - request_rows
    inverse = jnp.sum(jnp.where(one_hot, numbers[:, None], 0), axis=0)
    slot_start = jnp.cumsum(new_lengths, axis=1) - new_lengths
    positions = jnp.arange(OWN_TOK, dtype=jnp.int32)
    slot_of_place = (
        jnp.sum((slot_start[:, :, None] <= positions[None, None, :]).astype(jnp.int32), axis=1) - 1
    )
    owner_ids = jnp.arange(dp_count, dtype=jnp.int32)[:, None]
    owner_rows = owner_ids * per_owner + slot_of_place
    start_in_slot = jnp.take_along_axis(slot_start, slot_of_place, axis=1)
    source_rows = (
        jnp.take(offsets, jnp.take(inverse, owner_rows)) + positions[None, :] - start_in_slot
    )
    outgoing = jnp.take(prefill_latent, source_rows.reshape(-1), axis=0).reshape(
        dp_count, OWN_TOK, latent_width
    )
    incoming = lax.all_to_all(outgoing, "dp", split_axis=0, concat_axis=0, tiled=True)
    new_rows = incoming.reshape(dp_count * OWN_TOK, latent_width)
    my_lengths = lax.dynamic_index_in_dim(new_lengths, dp_rank, 0, keepdims=False)
    my_start = jnp.cumsum(my_lengths) - my_lengths
    in_slot = (positions[None, :] >= my_start[:, None]) & (
        positions[None, :] < (my_start + my_lengths)[:, None]
    )
    new_mask = jnp.tile(in_slot, (1, dp_count))
    cache_mask = jnp.arange(kv_cache.shape[1], dtype=jnp.int32)[None, :] < ctx_lengths[:, None]
    share_first = tp_rank * share_width

    def finish(first, last):
        step_ids = jnp.arange(first, last, dtype=jnp.int32)
        steps_here = last - first
        head_out = attend(
            queries[first:last],
            step_ids,
            kv_cache,
            cache_mask,
            new_rows,
            new_mask,
            step_latents,
            w_uv,
        )
        every_row = lax.all_gather(head_out, "dp", axis=1, tiled=True)
        partial_value = jnp.dot(
            every_row.reshape(steps_here * total_requests, -1),
            w_out.reshape(-1, block_width),
            preferred_element_type=jnp.float32,
        )
        partial_value = partial_value.reshape(steps_here, total_requests, block_width)
        own_cols = lax.dynamic_slice_in_dim(partial_value, share_first, share_width, 2) + hidden[
            first:last
        ].astype(jnp.float32)
        partial_value = lax.dynamic_update_slice_in_dim(partial_value, own_cols, share_first, 2)
        mixed = lax.psum_scatter(partial_value, "tp", scatter_dimension=2, tiled=True)
        squares = lax.psum(jnp.sum(mixed * mixed, axis=-1), ("dp", "tp"))
        gain_part = lax.dynamic_slice_in_dim(
            ffn_gain, dp_rank * block_width + share_first, share_width
        )
        normed_part = (
            mixed * lax.rsqrt(squares / model_width + norm_eps)[..., None] * gain_part
        ).astype(jnp.bfloat16)
        normed = lax.all_gather(normed_part, ("dp", "tp"), axis=2, tiled=True)
        flat_input = normed.reshape(steps_here * total_requests, model_width)
        gate_out = jnp.dot(flat_input, w_gate, preferred_element_type=jnp.float32)
        up_out = jnp.dot(flat_input, w_up, preferred_element_type=jnp.float32)
        activated = (jax.nn.silu(gate_out) * up_out).astype(jnp.bfloat16)
        down_out = jnp.dot(activated, w_down, preferred_element_type=jnp.float32).reshape(
            steps_here, total_requests, model_width
        )
        ffn_part = lax.psum_scatter(down_out, ("dp", "tp"), scatter_dimension=2, tiled=True)
        return (mixed + ffn_part).astype(jnp.bfloat16)

    step_total = queries.shape[0]
    result = jnp.concatenate([finish(index, index + 1) for index in range(step_total)], axis=0)
    return result


def solution(mesh):
    return jax.shard_map(
        shards,
        mesh=mesh,
        in_specs=(
            P("dp", None),
            P(),
            P(),
            P("dp"),
            P("dp", None, None),
            P(None, "dp", "tp", None),
            P(None, "dp", None),
            P("tp", None, None),
            P("tp", None, "dp"),
            P(None, None, ("dp", "tp")),
            P(),
            P(None, ("dp", "tp")),
            P(None, ("dp", "tp")),
            P(("dp", "tp"), None),
        ),
        out_specs=P(None, None, ("dp", "tp")),
        check_vma=False,
    )
```

profile of v0, /device:TPU:0, one launch (start us, length us, event | category | flops | bytes accessed | tf_op | source)
XLA Modules:
  0.0 562.0 jit_solution(4577492493033524395)
XLA Ops:
  11.7 1.2 gather_fusion.3
  13.1 1.5 gather_fusion.1
  16.6 7.3 %all-to-all-start = ((bf16[8,16,576]{2,1,0:T(8,128)(2,1)}), bf16[8,16,576]{2,1,0:T(8,128)(2,1)S(1)}, u32[]{:S(2)}, u32[]{:S(2)}) async-start(bf16[8,16,576]{2,1,0:T(8,128)(2,1)} %broadcast_select_fusion), calls=%async_computation | async-start | bytes 327680 | tf_op jit(solution)/shard_map/all_to_all | solution.py:108
  24.1 3.5 fusion.117
  29.6 1.9 all-to-all-done
  32.8 4.2 fusion.18
  37.9 30.9 %all_gather.12 = bf16[1,32,32,128]{3,2,0,1:T(8,128)(2,1)S(1)} all-gather(bf16[1,4,32,128]{3,2,0,1:T(8,128)(2,1)S(1)} %copy.84), channel_id=1, replica_groups=mesh['dp'=8,'tp'=4] {'dp'}, dimensions={1}, use_global_device_ids=true | all-gather | bytes 294912 | tf_op jit(solution)/shard_map/all_gather | solution.py:132
  69.6 1.4 fusion.21
  71.9 30.7 %all_gather.14 = bf16[1,32,32,128]{3,2,0,1:T(8,128)(2,1)S(1)} all-gather(bf16[1,4,32,128]{3,2,0,1:T(8,128)(2,1)S(1)} %copy.90), channel_id=1, replica_groups=mesh['dp'=8,'tp'=4] {'dp'}, dimensions={1}, use_global_device_ids=true | all-gather | bytes 294912 | tf_op jit(solution)/shard_map/all_gather | solution.py:132
  102.6 1.2 fusion.55
  103.9 1.2 fusion.52
  109.2 18.6 %reduce-scatter.13.cloned.1.call-done = f32[224,32]{1,0:T(8,128)} async-done(((f32[896,32]{1,0:T(8,128)}), f32[224,32]{1,0:T(8,128)}) %reduce-scatter.13.cloned.1.call-update) | async-done | bytes 28688
  128.9 22.7 %reduce-scatter.17.cloned.1.call-done = f32[224,32]{1,0:T(8,128)} async-done(((f32[896,32]{1,0:T(8,128)}), f32[224,32]{1,0:T(8,128)}) %reduce-scatter.17.cloned.1.call-update) | async-done | bytes 28688
  152.7 39.6 %all-reduce = (f32[1,32]{1,0:T(1,128)S(1)}, f32[1,32]{1,0:T(1,128)S(1)}) all-reduce(f32[1,32]{1,0:T(1,128)S(1)} %bitcast.267, f32[1,32]{1,0:T(1,128)S(1)} %bitcast.266), channel_id=1, replica_groups=mesh['dp'=8,'tp'=4] {'dp','tp'}, use_global_device_ids=true, to_apply=%region_24.26 | all-reduce | flops 64 | bytes 512 | tf_op jit(solution)/shard_map/psum | solution.py:144
  192.5 57.5 %all_gather.13 = bf16[1,32,7168]{1,0,2:T(2,128)(2,1)} all-gather(bf16[1,32,224]{1,0,2:T(2,128)(2,1)S(1)} %copy.85), channel_id=1, replica_groups=mesh['dp'=8,'tp'=4] {'dp','tp'}, dimensions={2}, use_global_device_ids=true | all-gather | bytes 473088 | tf_op jit(solution)/shard_map/all_gather | solution.py:151
  250.0 7.0 %copy.86 = bf16[1,32,7168]{2,1,0:T(8,128)(2,1)S(1)} copy(bf16[1,32,7168]{1,0,2:T(2,128)(2,1)} %all_gather.13) | data formatting | bytes 917504 | tf_op jit(solution)/shard_map/all_gather | solution.py:151
  256.9 5.8 %fusion.50 = f32[32,576]{1,0:T(8,128)S(1)} fusion(bf16[7168,576]{0,1:T(8,128)(2,1)} %param.27, bf16[1,32,7168]{2,1,0:T(8,128)(2,1)S(1)} %copy.86), kind=kOutput, calls=%fused_computation.64 | convolution fusion | flops 264241152 | bytes 8790016 | tf_op jit(solution)/shard_map/dot_general | solution.py:153
  262.7 12.5 %convolution_bitcast_fusion.1 = f32[7168,32]{1,0:T(8,128)} fusion(bf16[576,7168]{1,0:T(8,128)(2,1)} %param.29, bf16[7168,576]{0,1:T(8,128)(2,1)} %param.28, bf16[1,32,7168]{2,1,0:T(8,128)(2,1)S(1)} %copy.86, f32[32,576]{1,0:T(8,128)S(1)} %fusion.50), kind=kOutput, calls=%fused_computation.5 | convolution fusion | flops 528592896 | bytes 17965056 | tf_op jit(solution)/shard_map/dot_general | solution.py:156
  275.5 65.3 %all_gather.15 = bf16[1,32,7168]{1,0,2:T(2,128)(2,1)} all-gather(bf16[1,32,224]{1,0,2:T(2,128)(2,1)S(1)} %copy.91), channel_id=1, replica_groups=mesh['dp'=8,'tp'=4] {'dp','tp'}, dimensions={2}, use_global_device_ids=true | all-gather | bytes 473088 | tf_op jit(solution)/shard_map/all_gather | solution.py:151
  340.7 7.0 %copy.92 = bf16[1,32,7168]{2,1,0:T(8,128)(2,1)S(1)} copy(bf16[1,32,7168]{1,0,2:T(2,128)(2,1)} %all_gather.15) | data formatting | bytes 917504 | tf_op jit(solution)/shard_map/all_gather | solution.py:151
  347.7 5.9 %fusion.46 = f32[32,576]{1,0:T(8,128)S(1)} fusion(bf16[7168,576]{0,1:T(8,128)(2,1)} %param.27, bf16[1,32,7168]{2,1,0:T(8,128)(2,1)S(1)} %copy.92), kind=kOutput, calls=%fused_computation.61 | convolution fusion | flops 264241152 | bytes 8790016 | tf_op jit(solution)/shard_map/dot_general | solution.py:153
  353.6 12.6 %convolution_bitcast_fusion = f32[7168,32]{1,0:T(8,128)} fusion(bf16[576,7168]{1,0:T(8,128)(2,1)} %param.29, bf16[7168,576]{0,1:T(8,128)(2,1)} %param.28, bf16[1,32,7168]{2,1,0:T(8,128)(2,1)S(1)} %copy.92, f32[32,576]{1,0:T(8,128)S(1)} %fusion.46), kind=kOutput, calls=%fused_computation.4 | convolution fusion | flops 528592896 | bytes 17965056 | tf_op jit(solution)/shard_map/dot_general | solution.py:156
  366.2 50.0 %reduce-scatter.15.cloned.1.call-done = f32[224,32]{1,0:T(8,128)} async-done(((f32[7168,32]{1,0:T(8,128)}), f32[224,32]{1,0:T(8,128)}) %reduce-scatter.15.cloned.1.call-update) | async-done | bytes 28688
  417.2 136.6 %reduce-scatter.19.cloned.1.call-done = f32[224,32]{1,0:T(8,128)} async-done(((f32[7168,32]{1,0:T(8,128)}), f32[224,32]{1,0:T(8,128)}) %reduce-scatter.19.cloned.1.call-update) | async-done | bytes 28688
  (119 shorter events, 22.3 us)
Async XLA Ops:
  6.5 8.3 %copy-start.2 = (bf16[128,576]{0,1:T(8,128)(2,1)S(1)}, bf16[128,576]{0,1:T(8,128)(2,1)}, u32[]{:S(2)}) copy-start(bf16[128,576]{0,1:T(8,128)(2,1)} %param.16) | copy-start | bytes 442372
  9.9 14.0 %copy-start.6 = (s32[4]{0:T(128)S(1)}, s32[4]{0:T(128)}, u32[]{:S(2)}) copy-start(s32[4]{0:T(128)} %param.19) | copy-start | bytes 52
  9.9 14.1 %copy-start.1 = (bf16[2,4,32,576]{3,2,1,0:T(8,128)(2,1)S(1)}, bf16[2,4,32,576]{3,2,1,0:T(8,128)(2,1)}, u32[]{:S(2)}) copy-start(bf16[2,4,32,576]{3,2,1,0:T(8,128)(2,1)} %param.21) | copy-start | bytes 884740
  13.1 14.5 %slice-start = ((s8[4718592]{0:T(1024)(128)(4,1)}), s8[524288]{0:T(1024)(128)(4,1)S(1)}, s32[]{:S(2)}) async-start(s8[4718592]{0:T(1024)(128)(4,1)} %bitcast.242), calls=%async_computation.9 | async-start | bytes 1048576
  16.6 14.8 %all-to-all-start = ((bf16[8,16,576]{2,1,0:T(8,128)(2,1)}), bf16[8,16,576]{2,1,0:T(8,128)(2,1)S(1)}, u32[]{:S(2)}, u32[]{:S(2)}) async-start(bf16[8,16,576]{2,1,0:T(8,128)(2,1)} %broadcast_select_fusion), calls=%async_computation | async-start | bytes 327680 | tf_op jit(solution)/shard_map/all_to_all | solution.py:108
  23.9 103.9 %reduce-scatter.13.cloned.1.call-start = ((), (), s32[]{:S(2)}) async-start(), calls=%async_computation.5 | async-start | bytes 573440
  24.0 3.6 slice-start.1
  24.1 4.6 copy-start.4
  24.1 5.0 copy-start.5
  31.5 5.7 %copy-start = (bf16[32,512,128]{2,1,0:T(8,128)(2,1)S(1)}, bf16[32,512,128]{2,1,0:T(8,128)(2,1)}, u32[]{:S(2)}) copy-start(bf16[32,512,128]{2,1,0:T(8,128)(2,1)} %param.23) | copy-start | bytes 12582916
  31.5 38.0 %slice-start.2 = ((s8[4718592]{0:T(1024)(128)(4,1)}), s8[4194304]{0:T(1024)(128)(4,1)S(1)}, s32[]{:S(2)}) async-start(s8[4718592]{0:T(1024)(128)(4,1)} %bitcast.244), calls=%async_computation.11 | async-start | bytes 8388608
  32.8 36.8 %slice-start.3 = ((s8[4718592]{0:T(1024)(128)(4,1)}), s8[524288]{0:T(1024)(128)(4,1)S(1)}, s32[]{:S(2)}) async-start(s8[4718592]{0:T(1024)(128)(4,1)} %bitcast.244), calls=%async_computation.12 | async-start | bytes 1048576
  37.9 64.8 %slice-start.4 = ((s8[7340032]{0:T(1024)(128)(4,1)}), s8[4194304]{0:T(1024)(128)(4,1)S(1)}, s32[]{:S(2)}) async-start(s8[7340032]{0:T(1024)(128)(4,1)} %bitcast.246), calls=%async_computation.13 | async-start | bytes 8388608
  69.5 33.1 %slice-start.5 = ((s8[7340032]{0:T(1024)(128)(4,1)}), s8[3145728]{0:T(1024)(128)(4,1)S(1)}, s32[]{:S(2)}) async-start(s8[7340032]{0:T(1024)(128)(4,1)} %bitcast.246), calls=%async_computation.14 | async-start | bytes 6291456
  102.6 2.5 copy-start.3
  106.8 44.8 %reduce-scatter.17.cloned.1.call-start = ((), (), s32[]{:S(2)}) async-start(), calls=%async_computation.7 | async-start | bytes 573440
  108.4 307.9 %reduce-scatter.15.cloned.1.call-start = ((), (), s32[]{:S(2)}) async-start(), calls=%async_computation.6 | async-start | bytes 3784704
  275.3 278.5 %reduce-scatter.19.cloned.1.call-start = ((), (), s32[]{:S(2)}) async-start(), calls=%async_computation.8 | async-start | bytes 3784704
Sparse Core Ops, SparseCore 0:
  106.9 20.9 reduce-scatter.12
  130.3 21.1 reduce-scatter.16
  275.4 140.7 reduce-scatter.14
  418.5 135.2 reduce-scatter.18
where the time goes:
time: 563 us; the launch traced here: 562 us
  waiting for transfers between devices  230 us (41%)
  blocking collectives  224 us (40%)
  matrix products  52.5 us (9%)
  local copies, waits for them, and re-layouts  28.8 us (5%)
  between operations  13.6 us (2%)
  starting transfers between devices  7.44 us (1%)
  other arithmetic  5.77 us (1%)
    unnamed x8, waiting for transfers between devices  228 us
    all_gather x2, blocking collectives, finish(): normed = lax.all_gather(normed_part, ('dp', 'tp'), axis=2, tiled=True)  123 us
    all_gather x2, blocking collectives, finish(): every_row = lax.all_gather(head_out, 'dp', axis=1, tiled=True)  61.7 us
    psum x1, blocking collectives, finish(): squares = lax.psum(jnp.sum(mixed * mixed, axis=-1), ('dp', 'tp'))  39.6 us
    dot_general x2, matrix products, finish(): jnp.dot(activated, w_down, preferred_element_type=jnp.float32)  25.2 us
    all_gather x2, local copies, waits for them, and re-layouts, finish(): normed = lax.all_gather(normed_part, ('dp', 'tp'), axis=2, tiled=True)  14 us
    dot_general x2, matrix products, finish(): gate_out = jnp.dot(flat_input, w_gate, preferred_element_type=jnp.float32)  11.7 us
  transfers between devices with their start and end apart: 5, of which 5 were waited for; matrix products, arithmetic and copies ran while one was open for 6% of the time, Pallas kernels for 0%

commit v1 on v0

--- a/solution.py
+++ b/solution.py
@@ -1,6 +1,10 @@
+import functools
+
 import jax
 import jax.numpy as jnp
 from jax import lax
+from jax.experimental import pallas as pl
+from jax.experimental.pallas import tpu as pltpu
 from jax.sharding import PartitionSpec as P
 
 LAT = 512
@@ -60,7 +64,7 @@
     ).astype(jnp.bfloat16)
 
 
-def shards(
+def plain_shards(
     prefill_latent,
     request_slot,
     new_lengths,
@@ -145,13 +149,12 @@
         gain_part = lax.dynamic_slice_in_dim(
             ffn_gain, dp_rank * block_width + share_first, share_width
         )
-        normed_part = (
-            mixed * lax.rsqrt(squares / model_width + norm_eps)[..., None] * gain_part
-        ).astype(jnp.bfloat16)
-        normed = lax.all_gather(normed_part, ("dp", "tp"), axis=2, tiled=True)
-        flat_input = normed.reshape(steps_here * total_requests, model_width)
-        gate_out = jnp.dot(flat_input, w_gate, preferred_element_type=jnp.float32)
-        up_out = jnp.dot(flat_input, w_up, preferred_element_type=jnp.float32)
+        scaled_part = (mixed * gain_part).astype(jnp.bfloat16)
+        scaled = lax.all_gather(scaled_part, ("dp", "tp"), axis=2, tiled=True)
+        flat_input = scaled.reshape(steps_here * total_requests, model_width)
+        row_scale = lax.rsqrt(squares / model_width + norm_eps).reshape(-1, 1)
+        gate_out = jnp.dot(flat_input, w_gate, preferred_element_type=jnp.float32) * row_scale
+        up_out = jnp.dot(flat_input, w_up, preferred_element_type=jnp.float32) * row_scale
         activated = (jax.nn.silu(gate_out) * up_out).astype(jnp.bfloat16)
         down_out = jnp.dot(activated, w_down, preferred_element_type=jnp.float32).reshape(
             steps_here, total_requests, model_width
@@ -159,14 +162,668 @@
         ffn_part = lax.psum_scatter(down_out, ("dp", "tp"), scatter_dimension=2, tiled=True)
         return (mixed + ffn_part).astype(jnp.bfloat16)
 
-    step_total = queries.shape[0]
-    result = jnp.concatenate([finish(index, index + 1) for index in range(step_total)], axis=0)
-    return result
+    return finish(0, queries.shape[0])
+
+
+Z_COUNT, Y_COUNT, X_COUNT, CORES = 4, 2, 2, 2
+CHUNKS = 4
+PIECE = 256
+
+
+def dot_f32(left, right):
+    return jnp.dot(left, right, preferred_element_type=jnp.float32)
+
+
+def dot_rows(left, right):
+    return lax.dot_general(
+        left, right, (((1,), (1,)), ((), ())), preferred_element_type=jnp.float32
+    )
+
+
+def split_pieces(block, share):
+    pieces = []
+    for index in range(4):
+        first = index * share
+        base = first // 128 * 128
+        last = min(block.shape[1], -(-(first + PIECE) // 128) * 128)
+        window = block[:, base:last]
+        width = last - base
+        if first != base:
+            window = pltpu.roll(window, width - (first - base), 1)
+        pieces.append(window[:, :PIECE])
+    return pieces
+
+
+def layer_kernel(
+    slot_s,
+    len_s,
+    ctx_s,
+    pre_h,
+    kv_h,
+    qry_h,
+    stp_h,
+    uv_h,
+    wo_h,
+    hid_h,
+    gain_v,
+    wg_h,
+    wu_h,
+    wd_h,
+    out_ref,
+    pre,
+    kv,
+    qry,
+    stp,
+    uv,
+    wo,
+    hid,
+    wg,
+    wu,
+    wd,
+    tail,
+    outg,
+    score,
+    lat,
+    hbuf,
+    cpart,
+    csend,
+    crecv,
+    hidf,
+    mixed_v,
+    xbuf,
+    gacc,
+    uacc,
+    sqacc,
+    act,
+    e1s,
+    e1r,
+    keep1,
+    e2s,
+    e2r,
+    keep2,
+    e3s,
+    e3r,
+    e4s,
+    e4r,
+    load_sem,
+    a_send,
+    a_recv,
+    b_send,
+    b_recv,
+    c_send,
+    c_recv,
+    d_send,
+    d_recv,
+    e1_send,
+    e1_recv,
+    e2_send,
+    e2_recv,
+    e3_send,
+    e3_recv,
+    e4_send,
+    e4_recv,
+):
+    f32, bf16 = jnp.float32, jnp.bfloat16
+    dp_count = Z_COUNT * Y_COUNT
+    d = lax.axis_index("dp")
+    t = lax.axis_index("tp")
+    z, y = lax.div(d, Y_COUNT), lax.rem(d, Y_COUNT)
+    x, c = lax.div(t, CORES), lax.rem(t, CORES)
+    heads = qry.shape[2]
+    share = hid.shape[2]
+    block_width = 4 * share
+    rows = 2 * 4 * dp_count
+    y_peer = (z * Y_COUNT + (1 - y), t)
+    x_peer = (d, (1 - x) * CORES + c)
+    core_peer = (d, x * CORES + (1 - c))
+
+    def z_at(step):
+        return lax.rem(z + step, Z_COUNT)
+
+    def send(src, dst, send_sem, recv_sem, device):
+        copy = pltpu.make_async_remote_copy(
+            src_ref=src,
+            dst_ref=dst,
+            send_sem=send_sem,
+            recv_sem=recv_sem,
+            device_id=device,
+            device_id_type=pl.DeviceIdType.MESH,
+        )
+        copy.start()
+
+    def arrived(ref, sem):
+        pltpu.make_async_remote_copy(
+            src_ref=ref,
+            dst_ref=ref,
+            send_sem=sem,
+            recv_sem=sem,
+            device_id=y_peer,
+            device_id_type=pl.DeviceIdType.MESH,
+        ).wait_recv()
+
+    def sent(ref, sem):
+        pltpu.make_async_remote_copy(
+            src_ref=ref,
+            dst_ref=ref,
+            send_sem=sem,
+            recv_sem=sem,
+            device_id=y_peer,
+            device_id_type=pl.DeviceIdType.MESH,
+        ).wait_send()
+
+    barrier = pltpu.get_barrier_semaphore()
+    for step in range(1, dp_count):
+        pl.semaphore_signal(
+            barrier,
+            inc=1,
+            device_id=(lax.rem(d + step, dp_count), t),
+            device_id_type=pl.DeviceIdType.MESH,
+        )
+    for step in range(1, 4):
+        pl.semaphore_signal(
+            barrier,
+            inc=1,
+            device_id=(d, lax.rem(t + step, 4)),
+            device_id_type=pl.DeviceIdType.MESH,
+        )
+
+    def load(index, src, dst):
+        copy = pltpu.make_async_copy(src, dst, load_sem.at[index])
+        copy.start()
+        return copy
+
+    load_pre = load(0, pre_h, pre)
+    load_stp = load(1, stp_h, stp)
+    load_qry = load(2, qry_h, qry)
+    load_kv = [load(3 + i, kv_h.at[i], kv.at[i]) for i in range(4)]
+    load_hid = load(7, hid_h, hid)
+    load_uv = load(8, uv_h, uv)
+    load_wo = load(9, wo_h, wo)
+    load_wg = load(10, wg_h, wg)
+    load_wu = load(11, wu_h, wu)
+    load_wd = load(12, wd_h, wd)
+
+    pf_rows = pre.shape[0]
+    source = lax.broadcasted_iota(jnp.int32, (8, pf_rows), 1)
+
+    def place_request(r, carry):
+        dest, offset = carry
+        owner_row = slot_s[r]
+        owner = lax.shift_right_logical(owner_row, 2)
+        place = owner_row & 3
+        count = len_s[owner, place]
+        start = jnp.int32(0)
+        for k in range(3):
+            start = start + jnp.where(place > k, len_s[owner, k], 0)
+        inside = (source >= offset) & (source < offset + count)
+        dest = jnp.where(inside, source + (owner * OWN_TOK + start - offset), dest)
+        return dest, offset + count
+
+    dest, _ = lax.fori_loop(
+        0, 4 * dp_count, place_request, (jnp.full((8, pf_rows), -1, jnp.int32), jnp.int32(0))
+    )
+    target = lax.broadcasted_iota(jnp.int32, (pf_rows, pf_rows), 0)
+    pick = jnp.where(target == dest[0:1], 1.0, 0.0).astype(bf16)
+    load_pre.wait()
+    outg[...] = dot_f32(pick, pre[...]).astype(bf16)
+    pl.semaphore_wait(barrier, dp_count - 1 + 3)
+
+    def own_rows(index):
+        return pl.ds(pl.multiple_of(index * OWN_TOK, OWN_TOK), OWN_TOK)
+
+    for step in range(1, dp_count):
+        other = lax.rem(d + step, dp_count)
+        send(
+            outg.at[own_rows(other)],
+            tail.at[own_rows(d)],
+            a_send.at[step],
+            a_recv.at[d],
+            (other, t),
+        )
+    tail[own_rows(d), :] = outg[own_rows(d), :]
+    load_stp.wait()
+    tokens = jnp.concatenate(
+        [
+            stp[0].astype(f32),
+            stp[1].astype(f32),
+            jnp.zeros((tail.shape[0] - pf_rows - 8, stp.shape[2]), f32),
+        ],
+        axis=0,
+    )
+    tail[pf_rows:, :] = tokens.astype(bf16)
+
+    load_qry.wait()
+    key_block = 256
+    for i in range(4):
+        load_kv[i].wait()
+        query = jnp.concatenate([qry[0, i], qry[1, i]], axis=0)
+        for k in range(kv.shape[1] // key_block):
+            part = slice(k * key_block, (k + 1) * key_block)
+            score[i, :, part] = dot_rows(query, kv[i, part, :])
+
+    load_hid.wait()
+    hidf[...] = jnp.zeros_like(hidf)
+    hidf[0:32, 0:share] = hid[0].astype(f32)
+    hidf[32:64, 0:share] = hid[1].astype(f32)
+
+    for step in range(1, dp_count):
+        other = lax.rem(d + step, dp_count)
+        arrived(tail.at[own_rows(other)], a_recv.at[other])
+
+    scale = QKD ** (-0.5)
+    q_rows = 2 * heads
+    tail_col = lax.broadcasted_iota(jnp.int32, (q_rows, tail.shape[0]), 1)
+    tail_step = lax.broadcasted_iota(jnp.int32, (q_rows, tail.shape[0]), 0) // heads
+    spot = tail_col & (OWN_TOK - 1)
+    token = tail_col - pf_rows
+    key_col = lax.broadcasted_iota(jnp.int32, (q_rows, kv.shape[1]), 1)
+    start = jnp.int32(0)
+    for i in range(4):
+        count = len_s[d, i]
+        query = jnp.concatenate([qry[0, i], qry[1, i]], axis=0)
+        tail_score = dot_rows(query, tail[...]) * scale
+        fresh_ok = (tail_col < pf_rows) & (spot >= start) & (spot < start + count)
+        token_ok = (
+            (token >= 0)
+            & (token < 8)
+            & ((token & 3) == i)
+            & (lax.shift_right_arithmetic(token, 2) <= tail_step)
+        )
+        start = start + count
+        tail_score = jnp.where(fresh_ok | token_ok, tail_score, masked_score)
+        cache_score = jnp.where(key_col < ctx_s[i], score[i] * scale, masked_score)
+        highest = jnp.maximum(
+            jnp.max(cache_score, axis=1, keepdims=True), jnp.max(tail_score, axis=1, keepdims=True)
+        )
+        cache_exp = jnp.exp(cache_score - highest)
+        tail_exp = jnp.exp(tail_score - highest)
+        total = jnp.sum(cache_exp, axis=1, keepdims=True) + jnp.sum(
+            tail_exp, axis=1, keepdims=True
+        )
+        cache_prob = (cache_exp / total).astype(bf16)
+        tail_prob = (tail_exp / total).astype(bf16)
+        latent = dot_f32(cache_prob, kv[i, :, :LAT]) + dot_f32(tail_prob, tail[:, :LAT])
+        for s in range(2):
+            for b in range(LAT // 128):
+                lat[b, pl.ds(s * 4 + i, heads, stride=8), :] = latent[
+                    s * heads : (s + 1) * heads, b * 128 : (b + 1) * 128
+                ]
+
+    half = heads // 2
+    per_chunk = half // CHUNKS
+    load_uv.wait()
+
+    def head_rows(h):
+        return jnp.concatenate(
+            [lat[b, h * 8 : (h + 1) * 8, :] for b in range(LAT // 128)], axis=1
+        )
+
+    def forward_heads(chunk):
+        for step in range(1, Z_COUNT):
+            other = z_at(step) * Y_COUNT + y
+            arrived(hbuf.at[chunk, other], b_recv.at[chunk, other])
+            send(
+                hbuf.at[chunk, other],
+                hbuf.at[chunk, other],
+                b_send.at[chunk, 4 + step],
+                b_recv.at[chunk, other],
+                y_peer,
+            )
+
+    for chunk in range(CHUNKS):
+        outs = []
+        for p in range(per_chunk):
+            h = chunk * per_chunk + p
+            both = jnp.concatenate([head_rows(h), head_rows(h + half)], axis=0).astype(bf16)
+            low_out = dot_f32(both, uv[h])[0:8]
+            high_out = dot_f32(both, uv[h + half])[8:16]
+            outs.append(jnp.concatenate([low_out, high_out], axis=0).astype(bf16))
+        hbuf[chunk, d] = jnp.concatenate(outs, axis=1)
+        for step in range(1, Z_COUNT):
+            send(
+                hbuf.at[chunk, d],
+                hbuf.at[chunk, d],
+                b_send.at[chunk, step],
+                b_recv.at[chunk, d],
+                (z_at(step) * Y_COUNT + y, t),
+            )
+        send(
+            hbuf.at[chunk, d],
+            hbuf.at[chunk, d],
+            b_send.at[chunk, 0],
+            b_recv.at[chunk, d],
+            y_peer,
+        )
+        if chunk >= 1:
+            forward_heads(chunk - 1)
+    forward_heads(CHUNKS - 1)
+
+    load_wo.wait()
+    out_sum = None
+    for chunk in range(CHUNKS):
+        for step in range(Z_COUNT):
+            other = z_at(step) * Y_COUNT + (1 - y)
+            arrived(hbuf.at[chunk, other], b_recv.at[chunk, other])
+        left = hbuf[chunk].reshape(dp_count * 16, per_chunk * 128)
+        for a in range(2):
+            first = a * half + chunk * per_chunk
+            weight = wo[first : first + per_chunk].reshape(per_chunk * 128, block_width)
+            product = dot_f32(left, weight).reshape(dp_count, 16, block_width)
+            product = product[:, a * 8 : (a + 1) * 8, :]
+            out_sum = product if out_sum is None else out_sum + product
+    tiles = []
+    for s in range(2):
+        for k in range(dp_count // 2):
+            tiles.append(out_sum[2 * k, s * 4 : s * 4 + 4])
+            tiles.append(out_sum[2 * k + 1, s * 4 : s * 4 + 4])
+    partial = jnp.concatenate(tiles, axis=0)
+    for index, piece in enumerate(split_pieces(partial, share)):
+        cpart[index] = piece
+        csend[index] = piece.astype(bf16)
+    for step in range(1, 4):
+        other = lax.rem(t + step, 4)
+        send(csend.at[other], crecv.at[t], c_send.at[step], c_recv.at[t], (d, other))
+    mixed = cpart[t] + hidf[...]
+    for step in range(1, 4):
+        other = lax.rem(t + step, 4)
+        arrived(crecv.at[other], c_recv.at[other])
+        mixed = mixed + crecv[other].astype(f32)
+    lanes = lax.broadcasted_iota(jnp.int32, (rows, PIECE), 1)
+    mixed = jnp.where(lanes < share, mixed, 0.0)
+    mixed_v[...] = mixed
+    squares = jnp.sum(mixed * mixed, axis=1, keepdims=True)
+    squares_high = squares.astype(bf16).astype(f32)
+    own_block = mixed * gain_v[...]
+    own_block = jnp.where(lanes == share, squares_high, own_block)
+    own_block = jnp.where(lanes == share + 1, squares - squares_high, own_block)
+
+    def slot_of(cc, xx, yy, zz):
+        return ((cc * X_COUNT + xx) * Y_COUNT + yy) * Z_COUNT + zz
+
+    own = slot_of(c, x, y, z)
+    xbuf[own] = own_block.astype(bf16)
+
+    def pass_on(slot, kind, number, device):
+        send(xbuf.at[slot], xbuf.at[slot], d_send.at[kind, number], d_recv.at[slot], device)
+
+    for step in range(1, Z_COUNT):
+        pass_on(own, 0, step, (z_at(step) * Y_COUNT + y, t))
+    pass_on(own, 1, 0, y_peer)
+    pass_on(own, 2, 0, x_peer)
+    pass_on(own, 3, 0, core_peer)
+
+    gacc[...] = jnp.zeros_like(gacc)
+    uacc[...] = jnp.zeros_like(uacc)
+    sqacc[...] = jnp.zeros_like(sqacc)
+    load_wg.wait()
+    load_wu.wait()
+
+    def use_block(cc, xx, yy, zz):
+        slot = slot_of(cc, xx, yy, zz)
+        number = (zz * Y_COUNT + yy) * 4 + xx * CORES + cc
+        first = pl.multiple_of(number * share, 32)
+        block = xbuf[slot, :, 0:share]
+        gacc[...] += dot_f32(block, wg[pl.ds(first, share), :])
+        uacc[...] += dot_f32(block, wu[pl.ds(first, share), :])
+        sqacc[...] += xbuf[slot, :, 128:256].astype(f32)
+
+    def take(slot):
+        arrived(xbuf.at[slot], d_recv.at[slot])
+
+    use_block(c, x, y, z)
+
+    def from_z(step, carry):
+        zz = z_at(step)
+        slot = slot_of(c, x, y, zz)
+        take(slot)
+        pass_on(slot, 1, step, y_peer)
+        pass_on(slot, 2, step, x_peer)
+        pass_on(slot, 3, step, core_peer)
+        use_block(c, x, y, zz)
+        return carry
+
+    lax.fori_loop(1, Z_COUNT, from_z, 0)
+
+    def from_y(step, carry):
+        zz = z_at(step)
+        slot = slot_of(c, x, 1 - y, zz)
+        take(slot)
+        pass_on(slot, 2, 4 + step, x_peer)
+        pass_on(slot, 3, 4 + step, core_peer)
+        use_block(c, x, 1 - y, zz)
+        return carry
+
+    lax.fori_loop(0, Z_COUNT, from_y, 0)
+
+    def from_x(step, carry):
+        zz = z_at(step)
+        yy = lax.rem(y + lax.div(step, Z_COUNT), 2)
+        slot = slot_of(c, 1 - x, yy, zz)
+        take(slot)
+        pass_on(slot, 3, 8 + step, core_peer)
+        use_block(c, 1 - x, yy, zz)
+        return carry
+
+    lax.fori_loop(0, 2 * Z_COUNT, from_x, 0)
+
+    def from_core(step, carry):
+        zz = z_at(step)
+        yy = lax.rem(y + lax.div(step, Z_COUNT), 2)
+        xx = lax.rem(x + lax.div(step, 2 * Z_COUNT), 2)
+        slot = slot_of(1 - c, xx, yy, zz)
+        take(slot)
+        use_block(1 - c, xx, yy, zz)
+        return carry
+
+    lax.fori_loop(0, 4 * Z_COUNT, from_core, 0)
+
+    sq_lane = lax.broadcasted_iota(jnp.int32, sqacc.shape, 1) + 128
+    sq_here = (sq_lane == share) | (sq_lane == share + 1)
+    sq_total = jnp.sum(jnp.where(sq_here, sqacc[...], 0.0), axis=1, keepdims=True)
+    row_scale = lax.rsqrt(sq_total / (share * 4 * dp_count) + norm_eps)
+    gate = gacc[...] * row_scale
+    act[...] = (gate / (1.0 + jnp.exp(-gate)) * (uacc[...] * row_scale)).astype(bf16)
+
+    load_wd.wait()
+
+    def dest_dp(i):
+        yy = lax.rem(y + 1 + lax.div(i, Z_COUNT), 2)
+        return z_at(1 + lax.rem(i, Z_COUNT)) * Y_COUNT + yy
+
+    def over_x(i):
+        dd = dest_dp(i)
+        arrived(e1r.at[dd], e1_recv.at[dd])
+        e2s[dd] = (keep1[dd, 1 - x] + e1r[dd, 1 - x].astype(f32)).astype(bf16)
+        send(e2s.at[dd], e2r.at[dd], e2_send.at[dd], e2_recv.at[dd], x_peer)
+        keep2[dd] = keep1[dd, x] + e1r[dd, x].astype(f32)
+
+    def down(i, carry):
+        dd = dest_dp(i)
+        first = pl.multiple_of(dd * block_width, 128)
+        product = dot_f32(act[...], wd[:, pl.ds(first, block_width)])
+        pieces = split_pieces(product, share)
+        for xx in range(X_COUNT):
+            zero, one = pieces[2 * xx], pieces[2 * xx + 1]
+            keep1[dd, xx] = jnp.where(c == 0, zero, one)
+            e1s[dd, xx] = jnp.where(c == 0, one, zero).astype(bf16)
+        send(e1s.at[dd], e1r.at[dd], e1_send.at[dd], e1_recv.at[dd], core_peer)
+
+        @pl.when(i >= 2)
+        def _():
+            over_x(i - 2)
+
+        return carry
+
+    lax.fori_loop(0, dp_count, down, 0)
+    over_x(jnp.int32(dp_count - 2))
+    over_x(jnp.int32(dp_count - 1))
+    for k in range(Z_COUNT):
+        zz = z_at(1 + k)
+        dd = zz * Y_COUNT + (1 - y)
+        arrived(e2r.at[dd], e2_recv.at[dd])
+        e3s[zz] = (keep2[dd] + e2r[dd].astype(f32)).astype(bf16)
+        send(e3s.at[zz], e3r.at[zz], e3_send.at[zz], e3_recv.at[zz], y_peer)
+    result = mixed_v[...]
+    for k in range(Z_COUNT):
+        zz = z_at(1 + k)
+        dd = zz * Y_COUNT + y
+        arrived(e2r.at[dd], e2_recv.at[dd])
+        arrived(e3r.at[zz], e3_recv.at[zz])
+        value = keep2[dd] + e2r[dd].astype(f32) + e3r[zz].astype(f32)
+        if k < Z_COUNT - 1:
+            e4s[zz] = value.astype(bf16)
+            send(e4s.at[zz], e4r.at[z], e4_send.at[zz], e4_recv.at[z], (dd, t))
+        else:
+            result = result + value
+    for step in range(1, Z_COUNT):
+        other = z_at(step)
+        arrived(e4r.at[other], e4_recv.at[other])
+        result = result + e4r[other].astype(f32)
+    out_ref[0] = result[0:32, 0:share].astype(bf16)
+    out_ref[1] = result[32:64, 0:share].astype(bf16)
+
+    for step in range(1, dp_count):
+        sent(outg.at[own_rows(lax.rem(d + step, dp_count))], a_send.at[step])
+    for chunk in range(CHUNKS):
+        for number in range(8):
+            if number != 4:
+                sent(hbuf.at[chunk, d], b_send.at[chunk, number])
+    for step in range(1, 4):
+        sent(csend.at[lax.rem(t + step, 4)], c_send.at[step])
+    for kind, numbers in ((0, range(1, 4)), (1, range(4)), (2, range(8)), (3, range(16))):
+        for number in numbers:
+            sent(xbuf.at[own], d_send.at[kind, number])
+    for dd in range(dp_count):
+        sent(e1s.at[dd], e1_send.at[dd])
+        sent(e2s.at[dd], e2_send.at[dd])
+    for zz in range(Z_COUNT):
+        sent(e3s.at[zz], e3_send.at[zz])
+    for step in range(1, Z_COUNT):
+        sent(e4s.at[z_at(step)], e4_send.at[z_at(step)])
+
+
+def fused_shards(
+    prefill_latent,
+    request_slot,
+    new_lengths,
+    ctx_lengths,
+    kv_cache,
+    queries,
+    step_latents,
+    w_uv,
+    w_out,
+    hidden,
+    ffn_gain,
+    w_gate,
+    w_up,
+    w_down,
+):
+    f32, bf16 = jnp.float32, jnp.bfloat16
+    share = hidden.shape[2]
+    width = kv_cache.shape[2]
+    heads = queries.shape[2]
+    ff_share = w_gate.shape[1]
+    first = (lax.axis_index("dp") * 4 + lax.axis_index("tp")) * share
+    gain = lax.dynamic_slice_in_dim(ffn_gain, first, share)
+    gain = jnp.pad(gain, (0, PIECE - share)).reshape(1, PIECE)
+    smem = pl.BlockSpec(memory_space=pltpu.SMEM)
+    vmem = pl.BlockSpec(memory_space=pltpu.VMEM)
+    hbm = pl.BlockSpec(memory_space=pl.ANY)
+    dma = pltpu.SemaphoreType.DMA
+    pieces = (64, PIECE)
+    scratch = [
+        pltpu.VMEM(prefill_latent.shape, bf16),
+        pltpu.VMEM(kv_cache.shape, bf16),
+        pltpu.VMEM(queries.shape, bf16),
+        pltpu.VMEM(step_latents.shape, bf16),
+        pltpu.VMEM(w_uv.shape, bf16),
+        pltpu.VMEM(w_out.shape, bf16),
+        pltpu.VMEM(hidden.shape, bf16),
+        pltpu.VMEM(w_gate.shape, bf16),
+        pltpu.VMEM(w_up.shape, bf16),
+        pltpu.VMEM(w_down.shape, bf16),
+        pltpu.VMEM((prefill_latent.shape[0] + 128, width), bf16),
+        pltpu.VMEM(prefill_latent.shape, bf16),
+        pltpu.VMEM((4, 2 * heads, kv_cache.shape[1]), f32),
+        pltpu.VMEM((LAT // 128, heads * 8, 128), f32),
+        pltpu.VMEM((CHUNKS, 8, 16, heads // 2 // CHUNKS * 128), bf16),
+        pltpu.VMEM((4, *pieces), f32),
+        pltpu.VMEM((4, *pieces), bf16),
+        pltpu.VMEM((4, *pieces), bf16),
+        pltpu.VMEM(pieces, f32),
+        pltpu.VMEM(pieces, f32),
+        pltpu.VMEM((32, *pieces), bf16),
+        pltpu.VMEM((64, ff_share), f32),
+        pltpu.VMEM((64, ff_share), f32),
+        pltpu.VMEM((64, 128), f32),
+        pltpu.VMEM((64, ff_share), bf16),
+        pltpu.VMEM((8, 2, *pieces), bf16),
+        pltpu.VMEM((8, 2, *pieces), bf16),
+        pltpu.VMEM((8, 2, *pieces), f32),
+        pltpu.VMEM((8, *pieces), bf16),
+        pltpu.VMEM((8, *pieces), bf16),
+        pltpu.VMEM((8, *pieces), f32),
+        pltpu.VMEM((4, *pieces), bf16),
+        pltpu.VMEM((4, *pieces), bf16),
+        pltpu.VMEM((4, *pieces), bf16),
+        pltpu.VMEM((4, *pieces), bf16),
+        dma((16,)),
+        dma((8,)),
+        dma((8,)),
+        dma((CHUNKS, 8)),
+        dma((CHUNKS, 8)),
+        dma((4,)),
+        dma((4,)),
+        dma((4, 16)),
+        dma((32,)),
+        dma((8,)),
+        dma((8,)),
+        dma((8,)),
+        dma((8,)),
+        dma((4,)),
+        dma((4,)),
+        dma((4,)),
+        dma((4,)),
+    ]
+    return pl.pallas_call(
+        layer_kernel,
+        out_shape=jax.ShapeDtypeStruct(hidden.shape, bf16),
+        in_specs=[smem] * 3 + [hbm] * 7 + [vmem] + [hbm] * 3,
+        out_specs=vmem,
+        scratch_shapes=scratch,
+        compiler_params=pltpu.CompilerParams(
+            collective_id=0, has_side_effects=True, vmem_limit_bytes=60 * 1024 * 1024
+        ),
+        cost_estimate=pl.CostEstimate(
+            flops=4_000_000_000, bytes_accessed=42_000_000, transcendentals=400_000
+        ),
+    )(
+        request_slot,
+        new_lengths,
+        ctx_lengths,
+        prefill_latent,
+        kv_cache,
+        queries,
+        step_latents,
+        w_uv,
+        w_out,
+        hidden,
+        gain,
+        w_gate,
+        w_up,
+        w_down,
+    )
+
+
+def shards(dp_count, tp_count, *arrays):
+    if (dp_count, tp_count) == (Z_COUNT * Y_COUNT, X_COUNT * CORES):
+        return fused_shards(*arrays)
+    return plain_shards(*arrays)
 
 
 def solution(mesh):
     return jax.shard_map(
-        shards,
+        functools.partial(shards, mesh.shape["dp"], mesh.shape["tp"]),
         mesh=mesh,
         in_specs=(
             P("dp", None),

time: 563 us -> 99.6 us (0.18)
  waiting for transfers between devices: 230 us -> 0 us
  blocking collectives: 224 us -> 0 us
  Pallas kernels: 0 us -> 60.4 us
  matrix products: 52.5 us -> 0 us
  between operations: 13.6 us -> 0.01 us
  local copies, waits for them, and re-layouts: 28.8 us -> 38.2 us
  starting transfers between devices: 7.44 us -> 0 us
  other arithmetic: 5.77 us -> 0 us
    unnamed x8 -> x0, waiting for transfers between devices: 228 us -> none
    all_gather x4 -> x0, blocking collectives: 184 us -> none  [the longest x2 123 us: finish(): normed = lax.all_gather(normed_part, ('dp', 'tp'), axis=2, tiled=True)]
    pallas_call x0 -> x1, Pallas kernels: none -> 60.4 us  [fused_shards(): pl.pallas_call(layer_kernel, out_shape=jax.ShapeDtypeStruct(hidden.shape,...]
    dot_general x20 -> x0, matrix products: 52.5 us -> none  [the longest x2 25.2 us: finish(): jnp.dot(activated, w_down, preferred_element_type=jnp.float32)]
    psum x1 -> x0, blocking collectives: 39.6 us -> none  [finish(): squares = lax.psum(jnp.sum(mixed * mixed, axis=-1), ('dp', 'tp'))]
    unnamed x35 -> x6, local copies, waits for them, and re-layouts: 7.06 us -> 36.9 us
    all_gather x2 -> x0, local copies, waits for them, and re-layouts: 14 us -> none  [finish(): normed = lax.all_gather(normed_part, ('dp', 'tp'), axis=2, tiled=True)]
    all_to_all x1 -> x0, starting transfers between devices: 7.28 us -> none  [shards(): lax.all_to_all(outgoing, 'dp', split_axis=0, concat_axis=0, tiled=True)]
  transfers between devices with their start and end apart: 5 -> 0, of which waited for: 5 -> 0; matrix products, arithmetic and copies ran while one was open for 6% -> 0% of each run, Pallas kernels for 0% -> 0%
where the time goes in v1:
time: 99.6 us; the launch traced here: 98.6 us
  Pallas kernels  60.4 us (61%)
  local copies, waits for them, and re-layouts  38.2 us (38%)
    pallas_call x1, Pallas kernels, fused_shards(): pl.pallas_call(layer_kernel, out_shape=jax.ShapeDtypeStruct(hidden.shape,...  60.4 us
    unnamed x6, local copies, waits for them, and re-layouts  36.9 us

profile of v1, /device:TPU:0, one launch (start us, length us, event | category | flops | bytes accessed | tf_op | source)
XLA Modules:
  0.0 98.6 jit_solution(1434706734370487309)
XLA Ops:
  0.0 0.8 dynamic_slice.3
  0.8 0.5 pad.4
  1.3 1.3 %copy.15.len_s = s32[8,4]{1,0:T(8,128)} copy(s32[8,4]{0,1:T(4,128)} %param.16) | data formatting | bytes 256 | tf_op args[2]
  2.6 1.7 %copy.16.pre_h = bf16[128,576]{1,0:T(8,128)(2,1)} copy(bf16[128,576]{0,1:T(8,128)(2,1)} %param.14) | data formatting | bytes 294912 | tf_op args[0]
  4.3 7.7 %copy.17.kv_h = bf16[4,1024,576]{2,1,0:T(8,128)(2,1)} copy(bf16[4,1024,576]{1,2,0:T(8,128)(2,1)} %param.18) | data formatting | bytes 9437184 | tf_op args[4]
  12.0 12.4 %copy.18.wg_h = bf16[7168,576]{1,0:T(8,128)(2,1)} copy(bf16[7168,576]{0,1:T(8,128)(2,1)} %param.25) | data formatting | bytes 16515072 | tf_op args[11]
  24.4 12.4 %copy.19.wu_h = bf16[7168,576]{1,0:T(8,128)(2,1)} copy(bf16[7168,576]{0,1:T(8,128)(2,1)} %param.26) | data formatting | bytes 16515072 | tf_op args[12]
  36.8 60.4 %shard_map.136 = bf16[2,32,224]{2,1,0:T(8,128)(2,1)} custom-call(s32[32]{0:T(128)} %slot_s.1, s32[8,4]{1,0:T(8,128)} %copy.15.len_s, s32[4]{0:T(128)} %ctx_s.1, bf16[128,576]{1,0:T(8,128)(2,1)} %copy.16.pre_h, bf16[4,1024,576]{2,1,0:T(8,128)(2,1)} %copy.17.kv_h, bf16[2,4,32,576]{3,2,1,0:T(8,128)(2,1)} %qry_h.1, bf16[2,4,576]{2,1,0:T(4,128)(2,1)} %stp_h.1, ...), custom_call_target="tpu_custom_call" | custom-call | flops 4000000000 | bytes 42000000 | tf_op jit(solution)/shard_map/pallas_call | solution.py:788
  97.3 1.4 %copy.21 = bf16[2,32,224]{2,1,0:T(8,128)(2,1)} copy(bf16[2,32,224]{2,1,0:T(8,128)(2,1)} %shard_map.136) | data formatting | bytes 57344

commit v2 on v1

--- a/solution.py
+++ b/solution.py
@@ -167,7 +167,7 @@
 
 Z_COUNT, Y_COUNT, X_COUNT, CORES = 4, 2, 2, 2
 CHUNKS = 4
-PIECE = 256
+WINDOW = 512
 
 
 def dot_f32(left, right):
@@ -178,20 +178,6 @@
     return lax.dot_general(
         left, right, (((1,), (1,)), ((), ())), preferred_element_type=jnp.float32
     )
-
-
-def split_pieces(block, share):
-    pieces = []
-    for index in range(4):
-        first = index * share
-        base = first // 128 * 128
-        last = min(block.shape[1], -(-(first + PIECE) // 128) * 128)
-        window = block[:, base:last]
-        width = last - base
-        if first != base:
-            window = pltpu.roll(window, width - (first - base), 1)
-        pieces.append(window[:, :PIECE])
-    return pieces
 
 
 def layer_kernel(
@@ -228,7 +214,7 @@
     cpart,
     csend,
     crecv,
-    hidf,
+    hidw,
     mixed_v,
     xbuf,
     gacc,
@@ -245,6 +231,8 @@
     e3r,
     e4s,
     e4r,
+    fsend,
+    frecv,
     load_sem,
     a_send,
     a_recv,
@@ -262,6 +250,8 @@
     e3_recv,
     e4_send,
     e4_recv,
+    f_send,
+    f_recv,
 ):
     f32, bf16 = jnp.float32, jnp.bfloat16
     dp_count = Z_COUNT * Y_COUNT
@@ -338,12 +328,8 @@
     load_kv = [load(3 + i, kv_h.at[i], kv.at[i]) for i in range(4)]
     load_hid = load(7, hid_h, hid)
     load_uv = load(8, uv_h, uv)
-    load_wo = load(9, wo_h, wo)
-    load_wg = load(10, wg_h, wg)
-    load_wu = load(11, wu_h, wu)
-    load_wd = load(12, wd_h, wd)
-
-    pf_rows = pre.shape[0]
+
+    pf_rows = pre.shape[1]
     source = lax.broadcasted_iota(jnp.int32, (8, pf_rows), 1)
 
     def place_request(r, carry):
@@ -351,10 +337,10 @@
         owner_row = slot_s[r]
         owner = lax.shift_right_logical(owner_row, 2)
         place = owner_row & 3
-        count = len_s[owner, place]
+        count = len_s[place, owner]
         start = jnp.int32(0)
         for k in range(3):
-            start = start + jnp.where(place > k, len_s[owner, k], 0)
+            start = start + jnp.where(place > k, len_s[k, owner], 0)
         inside = (source >= offset) & (source < offset + count)
         dest = jnp.where(inside, source + (owner * OWN_TOK + start - offset), dest)
         return dest, offset + count
@@ -365,7 +351,7 @@
     target = lax.broadcasted_iota(jnp.int32, (pf_rows, pf_rows), 0)
     pick = jnp.where(target == dest[0:1], 1.0, 0.0).astype(bf16)
     load_pre.wait()
-    outg[...] = dot_f32(pick, pre[...]).astype(bf16)
+    outg[...] = dot_rows(pick, pre[...]).astype(bf16)
     pl.semaphore_wait(barrier, dp_count - 1 + 3)
 
     def own_rows(index):
@@ -397,14 +383,25 @@
     for i in range(4):
         load_kv[i].wait()
         query = jnp.concatenate([qry[0, i], qry[1, i]], axis=0)
-        for k in range(kv.shape[1] // key_block):
+        for k in range(kv.shape[2] // key_block):
             part = slice(k * key_block, (k + 1) * key_block)
-            score[i, :, part] = dot_rows(query, kv[i, part, :])
+            score[i, :, part] = dot_f32(query, kv[i, :, part])
+        if i == 1:
+            load_wo = load(9, wo_h, wo)
+    load_wg = load(10, wg_h, wg)
+    load_wu = load(11, wu_h, wu)
+    load_wd = load(12, wd_h, wd)
 
     load_hid.wait()
-    hidf[...] = jnp.zeros_like(hidf)
-    hidf[0:32, 0:share] = hid[0].astype(f32)
-    hidf[32:64, 0:share] = hid[1].astype(f32)
+    hidw[...] = jnp.zeros_like(hidw)
+    for s in range(2):
+        hidw[s, :, 0:share] = hid[s].astype(f32)
+    for s in range(2):
+        narrow = hidw[s]
+        placed = narrow
+        for k in range(1, 4):
+            placed = jnp.where(t == k, pltpu.roll(narrow, k * share, 1), placed)
+        hidw[s] = placed
 
     for step in range(1, dp_count):
         other = lax.rem(d + step, dp_count)
@@ -416,10 +413,10 @@
     tail_step = lax.broadcasted_iota(jnp.int32, (q_rows, tail.shape[0]), 0) // heads
     spot = tail_col & (OWN_TOK - 1)
     token = tail_col - pf_rows
-    key_col = lax.broadcasted_iota(jnp.int32, (q_rows, kv.shape[1]), 1)
+    key_col = lax.broadcasted_iota(jnp.int32, (q_rows, kv.shape[2]), 1)
     start = jnp.int32(0)
     for i in range(4):
-        count = len_s[d, i]
+        count = len_s[i, d]
         query = jnp.concatenate([qry[0, i], qry[1, i]], axis=0)
         tail_score = dot_rows(query, tail[...]) * scale
         fresh_ok = (tail_col < pf_rows) & (spot >= start) & (spot < start + count)
@@ -442,7 +439,8 @@
         )
         cache_prob = (cache_exp / total).astype(bf16)
         tail_prob = (tail_exp / total).astype(bf16)
-        latent = dot_f32(cache_prob, kv[i, :, :LAT]) + dot_f32(tail_prob, tail[:, :LAT])
+        cache_part = dot_rows(kv[i, 0:LAT, :], cache_prob)
+        latent = jnp.transpose(cache_part) + dot_f32(tail_prob, tail[:, :LAT])
         for s in range(2):
             for b in range(LAT // 128):
                 lat[b, pl.ds(s * 4 + i, heads, stride=8), :] = latent[
@@ -511,40 +509,59 @@
             product = dot_f32(left, weight).reshape(dp_count, 16, block_width)
             product = product[:, a * 8 : (a + 1) * 8, :]
             out_sum = product if out_sum is None else out_sum + product
-    tiles = []
+    partial = []
     for s in range(2):
-        for k in range(dp_count // 2):
-            tiles.append(out_sum[2 * k, s * 4 : s * 4 + 4])
-            tiles.append(out_sum[2 * k + 1, s * 4 : s * 4 + 4])
-    partial = jnp.concatenate(tiles, axis=0)
-    for index, piece in enumerate(split_pieces(partial, share)):
-        cpart[index] = piece
-        csend[index] = piece.astype(bf16)
+        tiles = []
+        for k in range(dp_count):
+            tiles.append(out_sum[k, s * 4 : s * 4 + 4])
+        partial.append(jnp.concatenate(tiles, axis=0) + hidw[s])
+    for xx in range(X_COUNT):
+        for cc in range(CORES):
+            piece = partial[cc][:, xx * 384 : xx * 384 + WINDOW]
+            cpart[xx * CORES + cc] = piece
+            csend[xx * CORES + cc] = piece.astype(bf16)
     for step in range(1, 4):
         other = lax.rem(t + step, 4)
         send(csend.at[other], crecv.at[t], c_send.at[step], c_recv.at[t], (d, other))
-    mixed = cpart[t] + hidf[...]
+    gain = jnp.concatenate(
+        [gain_v[pl.ds(d * (block_width // 128) + x * 3 + k, 1), :] for k in range(4)], axis=1
+    )
+    mixed = cpart[t]
     for step in range(1, 4):
         other = lax.rem(t + step, 4)
         arrived(crecv.at[other], c_recv.at[other])
         mixed = mixed + crecv[other].astype(f32)
-    lanes = lax.broadcasted_iota(jnp.int32, (rows, PIECE), 1)
-    mixed = jnp.where(lanes < share, mixed, 0.0)
+    lanes = lax.broadcasted_iota(jnp.int32, mixed.shape, 1)
+    pair = 2 * share
+    mixed = jnp.where((lanes >= 64 * x) & (lanes < 64 * x + pair), mixed, 0.0)
     mixed_v[...] = mixed
     squares = jnp.sum(mixed * mixed, axis=1, keepdims=True)
     squares_high = squares.astype(bf16).astype(f32)
-    own_block = mixed * gain_v[...]
-    own_block = jnp.where(lanes == share, squares_high, own_block)
-    own_block = jnp.where(lanes == share + 1, squares - squares_high, own_block)
-
-    def slot_of(cc, xx, yy, zz):
-        return ((cc * X_COUNT + xx) * Y_COUNT + yy) * Z_COUNT + zz
-
-    own = slot_of(c, x, y, z)
-    xbuf[own] = own_block.astype(bf16)
+    spare = pair * (1 - x)
+    own_block = mixed * gain
+    own_block = jnp.where(lanes == spare, squares_high, own_block)
+    own_block = jnp.where(lanes == spare + 1, squares - squares_high, own_block)
+
+    def place_of(n):
+        xx = lax.rem(x + lax.div(n, 2 * Z_COUNT), 2)
+        yy = lax.rem(y + lax.rem(lax.div(n, Z_COUNT), 2), 2)
+        return xx, yy, z_at(lax.rem(n, Z_COUNT))
+
+    def slot_of(n):
+        xx, yy, zz = place_of(n)
+        return (xx * Y_COUNT + yy) * Z_COUNT + zz
+
+    own = slot_of(jnp.int32(0))
+    xbuf[own, c] = own_block.astype(bf16)
 
     def pass_on(slot, kind, number, device):
-        send(xbuf.at[slot], xbuf.at[slot], d_send.at[kind, number], d_recv.at[slot], device)
+        send(
+            xbuf.at[slot, c],
+            xbuf.at[slot, c],
+            d_send.at[kind, number],
+            d_recv.at[slot * 2 + c],
+            device,
+        )
 
     for step in range(1, Z_COUNT):
         pass_on(own, 0, step, (z_at(step) * Y_COUNT + y, t))
@@ -557,72 +574,66 @@
     sqacc[...] = jnp.zeros_like(sqacc)
     load_wg.wait()
     load_wu.wait()
-
-    def use_block(cc, xx, yy, zz):
-        slot = slot_of(cc, xx, yy, zz)
-        number = (zz * Y_COUNT + yy) * 4 + xx * CORES + cc
-        first = pl.multiple_of(number * share, 32)
-        block = xbuf[slot, :, 0:share]
-        gacc[...] += dot_f32(block, wg[pl.ds(first, share), :])
-        uacc[...] += dot_f32(block, wu[pl.ds(first, share), :])
-        sqacc[...] += xbuf[slot, :, 128:256].astype(f32)
-
-    def take(slot):
-        arrived(xbuf.at[slot], d_recv.at[slot])
-
-    use_block(c, x, y, z)
-
-    def from_z(step, carry):
-        zz = z_at(step)
-        slot = slot_of(c, x, y, zz)
-        take(slot)
-        pass_on(slot, 1, step, y_peer)
-        pass_on(slot, 2, step, x_peer)
-        pass_on(slot, 3, step, core_peer)
-        use_block(c, x, y, zz)
+    block_lane = lax.broadcasted_iota(jnp.int32, (rows, WINDOW), 1)
+
+    def use_block(n):
+        xx, yy, zz = place_of(n)
+        slot = (xx * Y_COUNT + yy) * Z_COUNT + zz
+        arrived(xbuf.at[slot, 1 - c], d_recv.at[slot * 2 + (1 - c)])
+        block = xbuf[slot].reshape(rows, WINDOW).astype(f32)
+        inside = (block_lane >= 64 * xx) & (block_lane < 64 * xx + pair)
+        block = jnp.where(inside, block, 0.0).astype(bf16)
+        first = pl.multiple_of((zz * Y_COUNT + yy) * block_width + xx * 384, 128)
+        gacc[...] += dot_rows(wg[:, pl.ds(first, WINDOW)], block)
+        uacc[...] += dot_rows(wu[:, pl.ds(first, WINDOW)], block)
+        lane = pl.multiple_of(384 * (1 - xx), 128)
+        sqacc[xx] += xbuf[slot, :, :, pl.ds(lane, 128)].reshape(rows, 128).astype(f32)
+
+    def take(n):
+        slot = slot_of(n)
+        arrived(xbuf.at[slot, c], d_recv.at[slot * 2 + c])
+        return slot
+
+    def from_z(n, carry):
+        slot = take(n)
+        pass_on(slot, 1, n, y_peer)
+        pass_on(slot, 2, n, x_peer)
+        pass_on(slot, 3, n, core_peer)
         return carry
 
+    def from_y(n, carry):
+        slot = take(n)
+        pass_on(slot, 2, n, x_peer)
+        pass_on(slot, 3, n, core_peer)
+        use_block(n - 3)
+        return carry
+
+    def from_x(n, carry):
+        slot = take(n)
+        pass_on(slot, 3, n, core_peer)
+        use_block(n - 3)
+        return carry
+
+    def last(n, carry):
+        use_block(n)
+        return carry
+
+    use_block(jnp.int32(0))
     lax.fori_loop(1, Z_COUNT, from_z, 0)
-
-    def from_y(step, carry):
-        zz = z_at(step)
-        slot = slot_of(c, x, 1 - y, zz)
-        take(slot)
-        pass_on(slot, 2, 4 + step, x_peer)
-        pass_on(slot, 3, 4 + step, core_peer)
-        use_block(c, x, 1 - y, zz)
-        return carry
-
-    lax.fori_loop(0, Z_COUNT, from_y, 0)
-
-    def from_x(step, carry):
-        zz = z_at(step)
-        yy = lax.rem(y + lax.div(step, Z_COUNT), 2)
-        slot = slot_of(c, 1 - x, yy, zz)
-        take(slot)
-        pass_on(slot, 3, 8 + step, core_peer)
-        use_block(c, 1 - x, yy, zz)
-        return carry
-
-    lax.fori_loop(0, 2 * Z_COUNT, from_x, 0)
-
-    def from_core(step, carry):
-        zz = z_at(step)
-        yy = lax.rem(y + lax.div(step, Z_COUNT), 2)
-        xx = lax.rem(x + lax.div(step, 2 * Z_COUNT), 2)
-        slot = slot_of(1 - c, xx, yy, zz)
-        take(slot)
-        use_block(1 - c, xx, yy, zz)
-        return carry
-
-    lax.fori_loop(0, 4 * Z_COUNT, from_core, 0)
-
-    sq_lane = lax.broadcasted_iota(jnp.int32, sqacc.shape, 1) + 128
-    sq_here = (sq_lane == share) | (sq_lane == share + 1)
-    sq_total = jnp.sum(jnp.where(sq_here, sqacc[...], 0.0), axis=1, keepdims=True)
-    row_scale = lax.rsqrt(sq_total / (share * 4 * dp_count) + norm_eps)
-    gate = gacc[...] * row_scale
-    act[...] = (gate / (1.0 + jnp.exp(-gate)) * (uacc[...] * row_scale)).astype(bf16)
+    lax.fori_loop(Z_COUNT, 2 * Z_COUNT, from_y, 0)
+    lax.fori_loop(2 * Z_COUNT, 4 * Z_COUNT, from_x, 0)
+    lax.fori_loop(4 * Z_COUNT - 3, 4 * Z_COUNT, last, 0)
+
+    sq_lane = lax.broadcasted_iota(jnp.int32, (rows, 128), 1)
+    sq_all = jnp.where((sq_lane == pair - 384) | (sq_lane == pair - 383), sqacc[0], 0.0)
+    sq_all = sq_all + jnp.where(sq_lane < 2, sqacc[1], 0.0)
+    sq_total = jnp.sum(jnp.transpose(sq_all), axis=0, keepdims=True)
+    token_scale = lax.rsqrt(sq_total / (block_width * dp_count) + norm_eps)
+    gate = gacc[...] * token_scale
+    hidden_units = gate / (1.0 + jnp.exp(-gate)) * (uacc[...] * token_scale)
+    by_token = jnp.transpose(hidden_units)
+    act[0:32] = jnp.where(c == 0, by_token[0:32], by_token[32:64]).astype(bf16)
+    act[32:64] = jnp.where(c == 0, by_token[32:64], by_token[0:32]).astype(bf16)
 
     load_wd.wait()
 
@@ -641,11 +652,10 @@
         dd = dest_dp(i)
         first = pl.multiple_of(dd * block_width, 128)
         product = dot_f32(act[...], wd[:, pl.ds(first, block_width)])
-        pieces = split_pieces(product, share)
         for xx in range(X_COUNT):
-            zero, one = pieces[2 * xx], pieces[2 * xx + 1]
-            keep1[dd, xx] = jnp.where(c == 0, zero, one)
-            e1s[dd, xx] = jnp.where(c == 0, one, zero).astype(bf16)
+            window = slice(xx * 384, xx * 384 + WINDOW)
+            keep1[dd, xx] = product[0:32, window]
+            e1s[dd, xx] = product[32:64, window].astype(bf16)
         send(e1s.at[dd], e1r.at[dd], e1_send.at[dd], e1_recv.at[dd], core_peer)
 
         @pl.when(i >= 2)
@@ -679,8 +689,18 @@
         other = z_at(step)
         arrived(e4r.at[other], e4_recv.at[other])
         result = result + e4r[other].astype(f32)
-    out_ref[0] = result[0:32, 0:share].astype(bf16)
-    out_ref[1] = result[32:64, 0:share].astype(bf16)
+    halves = []
+    for cc in range(CORES):
+        near, far = cc * share, cc * share + 64
+        shifted = pltpu.roll(result, WINDOW - far, 1)
+        base = pltpu.roll(result, WINDOW - near, 1) if near else result
+        halves.append(jnp.where(x == 0, base, shifted)[:, 0:256].astype(bf16))
+    fsend[...] = jnp.where(c == 0, halves[1].astype(f32), halves[0].astype(f32)).astype(bf16)
+    send(fsend, frecv, f_send.at[0], f_recv.at[0], core_peer)
+    mine = jnp.where(c == 0, halves[0].astype(f32), halves[1].astype(f32)).astype(bf16)
+    out_ref[c] = mine[:, 0:share]
+    arrived(frecv, f_recv.at[0])
+    out_ref[1 - c] = frecv[:, 0:share]
 
     for step in range(1, dp_count):
         sent(outg.at[own_rows(lax.rem(d + step, dp_count))], a_send.at[step])
@@ -692,7 +712,7 @@
         sent(csend.at[lax.rem(t + step, 4)], c_send.at[step])
     for kind, numbers in ((0, range(1, 4)), (1, range(4)), (2, range(8)), (3, range(16))):
         for number in numbers:
-            sent(xbuf.at[own], d_send.at[kind, number])
+            sent(xbuf.at[own, c], d_send.at[kind, number])
     for dd in range(dp_count):
         sent(e1s.at[dd], e1_send.at[dd])
         sent(e2s.at[dd], e2_send.at[dd])
@@ -700,6 +720,7 @@
         sent(e3s.at[zz], e3_send.at[zz])
     for step in range(1, Z_COUNT):
         sent(e4s.at[z_at(step)], e4_send.at[z_at(step)])
+    sent(fsend, f_send.at[0])
 
 
 def fused_shards(
@@ -719,18 +740,20 @@
     w_down,
 ):
     f32, bf16 = jnp.float32, jnp.bfloat16
-    share = hidden.shape[2]
-    width = kv_cache.shape[2]
+    width = queries.shape[3]
     heads = queries.shape[2]
-    ff_share = w_gate.shape[1]
-    first = (lax.axis_index("dp") * 4 + lax.axis_index("tp")) * share
-    gain = lax.dynamic_slice_in_dim(ffn_gain, first, share)
-    gain = jnp.pad(gain, (0, PIECE - share)).reshape(1, PIECE)
+    ff_share = w_down.shape[0]
+    prefill_latent = prefill_latent.T
+    new_lengths = new_lengths.T
+    kv_cache = kv_cache.transpose(0, 2, 1)
+    w_gate = w_gate.T
+    w_up = w_up.T
+    gain = ffn_gain.reshape(-1, 128)
     smem = pl.BlockSpec(memory_space=pltpu.SMEM)
     vmem = pl.BlockSpec(memory_space=pltpu.VMEM)
     hbm = pl.BlockSpec(memory_space=pl.ANY)
     dma = pltpu.SemaphoreType.DMA
-    pieces = (64, PIECE)
+    pieces = (32, WINDOW)
     scratch = [
         pltpu.VMEM(prefill_latent.shape, bf16),
         pltpu.VMEM(kv_cache.shape, bf16),
@@ -742,20 +765,20 @@
         pltpu.VMEM(w_gate.shape, bf16),
         pltpu.VMEM(w_up.shape, bf16),
         pltpu.VMEM(w_down.shape, bf16),
-        pltpu.VMEM((prefill_latent.shape[0] + 128, width), bf16),
-        pltpu.VMEM(prefill_latent.shape, bf16),
-        pltpu.VMEM((4, 2 * heads, kv_cache.shape[1]), f32),
+        pltpu.VMEM((prefill_latent.shape[1] + 128, width), bf16),
+        pltpu.VMEM((prefill_latent.shape[1], width), bf16),
+        pltpu.VMEM((4, 2 * heads, kv_cache.shape[2]), f32),
         pltpu.VMEM((LAT // 128, heads * 8, 128), f32),
         pltpu.VMEM((CHUNKS, 8, 16, heads // 2 // CHUNKS * 128), bf16),
         pltpu.VMEM((4, *pieces), f32),
         pltpu.VMEM((4, *pieces), bf16),
         pltpu.VMEM((4, *pieces), bf16),
+        pltpu.VMEM((2, 32, w_out.shape[2]), f32),
         pltpu.VMEM(pieces, f32),
-        pltpu.VMEM(pieces, f32),
-        pltpu.VMEM((32, *pieces), bf16),
-        pltpu.VMEM((64, ff_share), f32),
-        pltpu.VMEM((64, ff_share), f32),
-        pltpu.VMEM((64, 128), f32),
+        pltpu.VMEM((16, 2, *pieces), bf16),
+        pltpu.VMEM((ff_share, 64), f32),
+        pltpu.VMEM((ff_share, 64), f32),
+        pltpu.VMEM((2, 64, 128), f32),
         pltpu.VMEM((64, ff_share), bf16),
         pltpu.VMEM((8, 2, *pieces), bf16),
         pltpu.VMEM((8, 2, *pieces), bf16),
@@ -767,6 +790,8 @@
         pltpu.VMEM((4, *pieces), bf16),
         pltpu.VMEM((4, *pieces), bf16),
         pltpu.VMEM((4, *pieces), bf16),
+        pltpu.VMEM((32, 256), bf16),
+        pltpu.VMEM((32, 256), bf16),
         dma((16,)),
         dma((8,)),
         dma((8,)),
@@ -784,6 +809,8 @@
         dma((4,)),
         dma((4,)),
         dma((4,)),
+        dma((1,)),
+        dma((1,)),
     ]
     return pl.pallas_call(
         layer_kernel,

time: 99.6 us -> 63.1 us (0.63)
  local copies, waits for them, and re-layouts: 38.2 us -> 1.38 us
  Pallas kernels: 60.4 us -> 61.4 us
    unnamed x6 -> x1, local copies, waits for them, and re-layouts: 36.9 us -> 1.38 us
where the time goes in v2:
time: 63.1 us; the launch traced here: 62.8 us
  Pallas kernels  61.4 us (97%)
  local copies, waits for them, and re-layouts  1.38 us (2%)
    pallas_call x1, Pallas kernels, fused_shards(): pl.pallas_call(layer_kernel, out_shape=jax.ShapeDtypeStruct(hidden.shape,...  61.4 us
    unnamed x1, local copies, waits for them, and re-layouts  1.38 us

profile of v2, /device:TPU:0, one launch (start us, length us, event | category | flops | bytes accessed | tf_op | source)
XLA Modules:
  0.0 62.8 jit_solution(14362428298356032040)
XLA Ops:
  0.0 61.4 %shard_map.136 = bf16[2,32,224]{2,1,0:T(8,128)(2,1)} custom-call(s32[32]{0:T(128)} %slot_s.1, s32[4,8]{1,0:T(4,128)} %bitcast.11, s32[4]{0:T(128)} %ctx_s.1, bf16[576,128]{1,0:T(8,128)(2,1)} %bitcast.9, bf16[4,576,1024]{2,1,0:T(8,128)(2,1)} %bitcast.8, bf16[2,4,32,576]{3,2,1,0:T(8,128)(2,1)} %qry_h.1, bf16[2,4,576]{2,1,0:T(4,128)(2,1)} %stp_h.1, ...), custom_call_target="tpu_custom_call" | custom-call | flops 4000000000 | bytes 42000000 | tf_op jit(solution)/shard_map/pallas_call | solution.py:815
  61.4 1.4 %copy.16 = bf16[2,32,224]{2,1,0:T(8,128)(2,1)} copy(bf16[2,32,224]{2,1,0:T(8,128)(2,1)} %shard_map.136) | data formatting | bytes 57344

commit v3 on v2

--- a/solution.py
+++ b/solution.py
@@ -233,6 +233,7 @@
     e4r,
     fsend,
     frecv,
+    cache_out,
     load_sem,
     a_send,
     a_recv,
@@ -403,44 +404,48 @@
             placed = jnp.where(t == k, pltpu.roll(narrow, k * share, 1), placed)
         hidw[s] = placed
 
+    scale = QKD ** (-0.5)
+    q_rows = 2 * heads
+    key_col = lax.broadcasted_iota(jnp.int32, (q_rows, kv.shape[2]), 1)
+    cache_max, cache_sum = [], []
+    for i in range(4):
+        cache_score = jnp.where(key_col < ctx_s[i], score[i] * scale, masked_score)
+        top = jnp.max(cache_score, axis=1, keepdims=True)
+        cache_exp = jnp.exp(cache_score - top)
+        cache_max.append(top)
+        cache_sum.append(jnp.sum(cache_exp, axis=1, keepdims=True))
+        cache_out[i] = jnp.transpose(dot_rows(kv[i, 0:LAT, :], cache_exp.astype(bf16)))
+
     for step in range(1, dp_count):
         other = lax.rem(d + step, dp_count)
         arrived(tail.at[own_rows(other)], a_recv.at[other])
 
-    scale = QKD ** (-0.5)
-    q_rows = 2 * heads
     tail_col = lax.broadcasted_iota(jnp.int32, (q_rows, tail.shape[0]), 1)
     tail_step = lax.broadcasted_iota(jnp.int32, (q_rows, tail.shape[0]), 0) // heads
     spot = tail_col & (OWN_TOK - 1)
     token = tail_col - pf_rows
-    key_col = lax.broadcasted_iota(jnp.int32, (q_rows, kv.shape[2]), 1)
+    token_place = token & 3
+    token_ok = (token >= 0) & (token < 8) & (lax.shift_right_arithmetic(token, 2) <= tail_step)
     start = jnp.int32(0)
     for i in range(4):
         count = len_s[i, d]
         query = jnp.concatenate([qry[0, i], qry[1, i]], axis=0)
         tail_score = dot_rows(query, tail[...]) * scale
         fresh_ok = (tail_col < pf_rows) & (spot >= start) & (spot < start + count)
-        token_ok = (
-            (token >= 0)
-            & (token < 8)
-            & ((token & 3) == i)
-            & (lax.shift_right_arithmetic(token, 2) <= tail_step)
-        )
         start = start + count
-        tail_score = jnp.where(fresh_ok | token_ok, tail_score, masked_score)
-        cache_score = jnp.where(key_col < ctx_s[i], score[i] * scale, masked_score)
-        highest = jnp.maximum(
-            jnp.max(cache_score, axis=1, keepdims=True), jnp.max(tail_score, axis=1, keepdims=True)
-        )
-        cache_exp = jnp.exp(cache_score - highest)
-        tail_exp = jnp.exp(tail_score - highest)
-        total = jnp.sum(cache_exp, axis=1, keepdims=True) + jnp.sum(
-            tail_exp, axis=1, keepdims=True
-        )
-        cache_prob = (cache_exp / total).astype(bf16)
-        tail_prob = (tail_exp / total).astype(bf16)
-        cache_part = dot_rows(kv[i, 0:LAT, :], cache_prob)
-        latent = jnp.transpose(cache_part) + dot_f32(tail_prob, tail[:, :LAT])
+        tail_score = jnp.where(
+            fresh_ok | (token_ok & (token_place == i)), tail_score, masked_score
+        )
+        tail_max = jnp.max(tail_score, axis=1, keepdims=True)
+        tail_exp = jnp.exp(tail_score - tail_max)
+        tail_sum = jnp.sum(tail_exp, axis=1, keepdims=True)
+        highest = jnp.maximum(cache_max[i], tail_max)
+        cache_part = jnp.exp(cache_max[i] - highest)
+        tail_part = jnp.exp(tail_max - highest)
+        total = cache_sum[i] * cache_part + tail_sum * tail_part
+        latent = cache_out[i] * (cache_part / total) + dot_f32(
+            tail_exp.astype(bf16), tail[:, :LAT]
+        ) * (tail_part / total)
         for s in range(2):
             for b in range(LAT // 128):
                 lat[b, pl.ds(s * 4 + i, heads, stride=8), :] = latent[
@@ -542,16 +547,10 @@
     own_block = jnp.where(lanes == spare, squares_high, own_block)
     own_block = jnp.where(lanes == spare + 1, squares - squares_high, own_block)
 
-    def place_of(n):
-        xx = lax.rem(x + lax.div(n, 2 * Z_COUNT), 2)
-        yy = lax.rem(y + lax.rem(lax.div(n, Z_COUNT), 2), 2)
-        return xx, yy, z_at(lax.rem(n, Z_COUNT))
-
-    def slot_of(n):
-        xx, yy, zz = place_of(n)
+    def slot_of(xx, yy, zz):
         return (xx * Y_COUNT + yy) * Z_COUNT + zz
 
-    own = slot_of(jnp.int32(0))
+    own = slot_of(x, y, z)
     xbuf[own, c] = own_block.astype(bf16)
 
     def pass_on(slot, kind, number, device):
@@ -576,9 +575,8 @@
     load_wu.wait()
     block_lane = lax.broadcasted_iota(jnp.int32, (rows, WINDOW), 1)
 
-    def use_block(n):
-        xx, yy, zz = place_of(n)
-        slot = (xx * Y_COUNT + yy) * Z_COUNT + zz
+    def use_block(xx, yy, zz):
+        slot = slot_of(xx, yy, zz)
         arrived(xbuf.at[slot, 1 - c], d_recv.at[slot * 2 + (1 - c)])
         block = xbuf[slot].reshape(rows, WINDOW).astype(f32)
         inside = (block_lane >= 64 * xx) & (block_lane < 64 * xx + pair)
@@ -589,40 +587,58 @@
         lane = pl.multiple_of(384 * (1 - xx), 128)
         sqacc[xx] += xbuf[slot, :, :, pl.ds(lane, 128)].reshape(rows, 128).astype(f32)
 
-    def take(n):
-        slot = slot_of(n)
+    def take(xx, yy, zz):
+        slot = slot_of(xx, yy, zz)
         arrived(xbuf.at[slot, c], d_recv.at[slot * 2 + c])
         return slot
 
-    def from_z(n, carry):
-        slot = take(n)
-        pass_on(slot, 1, n, y_peer)
-        pass_on(slot, 2, n, x_peer)
-        pass_on(slot, 3, n, core_peer)
+    def from_z(m, carry):
+        slot = take(x, y, z_at(m))
+        pass_on(slot, 1, m, y_peer)
+        pass_on(slot, 2, m, x_peer)
+        pass_on(slot, 3, m, core_peer)
         return carry
 
-    def from_y(n, carry):
-        slot = take(n)
-        pass_on(slot, 2, n, x_peer)
-        pass_on(slot, 3, n, core_peer)
-        use_block(n - 3)
+    def from_sides(m):
+        zz = z_at(m)
+        odd = lax.rem(zz, 2)
+        by_y = take(x, 1 - y, zz)
+
+        @pl.when(odd == 0)
+        def _():
+            pass_on(by_y, 2, 4 + lax.div(zz, 2), x_peer)
+
+        pass_on(by_y, 3, 4 + m, core_peer)
+        by_x = take(1 - x, y, zz)
+
+        @pl.when(odd == 1)
+        def _():
+            pass_on(by_x, 1, 4 + lax.div(zz, 2), y_peer)
+
+        pass_on(by_x, 3, 8 + m, core_peer)
+
+    def from_sides_and_use(m, carry):
+        from_sides(m)
+        use_block(x, y, z_at(m))
         return carry
 
-    def from_x(n, carry):
-        slot = take(n)
-        pass_on(slot, 3, n, core_peer)
-        use_block(n - 3)
+    def from_corner_and_use(m, carry):
+        zz = z_at(m)
+        pass_on(take(1 - x, 1 - y, zz), 3, 12 + m, core_peer)
+        use_block(x, 1 - y, zz)
+        use_block(1 - x, y, zz)
         return carry
 
-    def last(n, carry):
-        use_block(n)
+    def use_corner(m, carry):
+        use_block(1 - x, 1 - y, z_at(m))
         return carry
 
-    use_block(jnp.int32(0))
+    use_block(x, y, z)
     lax.fori_loop(1, Z_COUNT, from_z, 0)
-    lax.fori_loop(Z_COUNT, 2 * Z_COUNT, from_y, 0)
-    lax.fori_loop(2 * Z_COUNT, 4 * Z_COUNT, from_x, 0)
-    lax.fori_loop(4 * Z_COUNT - 3, 4 * Z_COUNT, last, 0)
+    from_sides(jnp.int32(0))
+    lax.fori_loop(1, Z_COUNT, from_sides_and_use, 0)
+    lax.fori_loop(0, Z_COUNT, from_corner_and_use, 0)
+    lax.fori_loop(0, Z_COUNT, use_corner, 0)
 
     sq_lane = lax.broadcasted_iota(jnp.int32, (rows, 128), 1)
     sq_all = jnp.where((sq_lane == pair - 384) | (sq_lane == pair - 383), sqacc[0], 0.0)
@@ -641,12 +657,32 @@
         yy = lax.rem(y + 1 + lax.div(i, Z_COUNT), 2)
         return z_at(1 + lax.rem(i, Z_COUNT)) * Y_COUNT + yy
 
-    def over_x(i):
+    def first_turn(i):
         dd = dest_dp(i)
+        zz = lax.div(dd, Y_COUNT)
+        odd = lax.rem(zz, 2)
         arrived(e1r.at[dd], e1_recv.at[dd])
-        e2s[dd] = (keep1[dd, 1 - x] + e1r[dd, 1 - x].astype(f32)).astype(bf16)
-        send(e2s.at[dd], e2r.at[dd], e2_send.at[dd], e2_recv.at[dd], x_peer)
-        keep2[dd] = keep1[dd, x] + e1r[dd, x].astype(f32)
+
+        def summed(xx):
+            return keep1[dd, xx] + e1r[dd, xx].astype(f32)
+
+        @pl.when(odd == 0)
+        def _():
+            e2s[dd] = summed(1 - x).astype(bf16)
+            send(e2s.at[dd], e2r.at[dd], e2_send.at[dd], e2_recv.at[dd], x_peer)
+            keep2[dd] = summed(x)
+
+        @pl.when((odd == 1) & (i < Z_COUNT))
+        def _():
+            for xx in range(X_COUNT):
+                k = zz * 2 + xx
+                e2s[k] = summed(xx).astype(bf16)
+                send(e2s.at[k], e2r.at[k], e2_send.at[k], e2_recv.at[k], y_peer)
+
+        @pl.when((odd == 1) & (i >= Z_COUNT))
+        def _():
+            for xx in range(X_COUNT):
+                keep2[zz * 2 + xx] = summed(xx)
 
     def down(i, carry):
         dd = dest_dp(i)
@@ -660,26 +696,36 @@
 
         @pl.when(i >= 2)
         def _():
-            over_x(i - 2)
+            first_turn(i - 2)
 
         return carry
 
     lax.fori_loop(0, dp_count, down, 0)
-    over_x(jnp.int32(dp_count - 2))
-    over_x(jnp.int32(dp_count - 1))
+    first_turn(jnp.int32(dp_count - 2))
+    first_turn(jnp.int32(dp_count - 1))
     for k in range(Z_COUNT):
         zz = z_at(1 + k)
-        dd = zz * Y_COUNT + (1 - y)
-        arrived(e2r.at[dd], e2_recv.at[dd])
-        e3s[zz] = (keep2[dd] + e2r[dd].astype(f32)).astype(bf16)
-        send(e3s.at[zz], e3r.at[zz], e3_send.at[zz], e3_recv.at[zz], y_peer)
+        odd = lax.rem(zz, 2)
+        sent_part = zz * 2 + (1 - y) + odd * (y - x)
+        arrived(e2r.at[sent_part], e2_recv.at[sent_part])
+        e3s[zz] = (keep2[sent_part] + e2r[sent_part].astype(f32)).astype(bf16)
+        peer_y = y + (1 - odd) * (1 - 2 * y)
+        peer_x = x + odd * (1 - 2 * x)
+        send(
+            e3s.at[zz],
+            e3r.at[zz],
+            e3_send.at[zz],
+            e3_recv.at[zz],
+            (z * Y_COUNT + peer_y, peer_x * CORES + c),
+        )
     result = mixed_v[...]
     for k in range(Z_COUNT):
         zz = z_at(1 + k)
         dd = zz * Y_COUNT + y
-        arrived(e2r.at[dd], e2_recv.at[dd])
+        kept_part = zz * 2 + y + lax.rem(zz, 2) * (x - y)
+        arrived(e2r.at[kept_part], e2_recv.at[kept_part])
         arrived(e3r.at[zz], e3_recv.at[zz])
-        value = keep2[dd] + e2r[dd].astype(f32) + e3r[zz].astype(f32)
+        value = keep2[kept_part] + e2r[kept_part].astype(f32) + e3r[zz].astype(f32)
         if k < Z_COUNT - 1:
             e4s[zz] = value.astype(bf16)
             send(e4s.at[zz], e4r.at[z], e4_send.at[zz], e4_recv.at[z], (dd, t))
@@ -710,7 +756,7 @@
                 sent(hbuf.at[chunk, d], b_send.at[chunk, number])
     for step in range(1, 4):
         sent(csend.at[lax.rem(t + step, 4)], c_send.at[step])
-    for kind, numbers in ((0, range(1, 4)), (1, range(4)), (2, range(8)), (3, range(16))):
+    for kind, numbers in ((0, range(1, 4)), (1, range(6)), (2, range(6)), (3, range(16))):
         for number in numbers:
             sent(xbuf.at[own, c], d_send.at[kind, number])
     for dd in range(dp_count):
@@ -792,6 +838,7 @@
         pltpu.VMEM((4, *pieces), bf16),
         pltpu.VMEM((32, 256), bf16),
         pltpu.VMEM((32, 256), bf16),
+        pltpu.VMEM((4, 2 * heads, LAT), f32),
         dma((16,)),
         dma((8,)),
         dma((8,)),

time: 63.1 us -> 62.2 us (0.986)
  Pallas kernels: 61.4 us -> 60.6 us
    pallas_call x1, Pallas kernels: 61.4 us -> 60.6 us  [fused_shards(): pl.pallas_call(layer_kernel, out_shape=jax.ShapeDtypeStruct(hidden.shape,...]
where the time goes in v3:
time: 62.2 us; the launch traced here: 62 us
  Pallas kernels  60.6 us (97%)
  local copies, waits for them, and re-layouts  1.38 us (2%)
    pallas_call x1, Pallas kernels, fused_shards(): pl.pallas_call(layer_kernel, out_shape=jax.ShapeDtypeStruct(hidden.shape,...  60.6 us
    unnamed x1, local copies, waits for them, and re-layouts  1.38 us

profile of v3, /device:TPU:0, one launch (start us, length us, event | category | flops | bytes accessed | tf_op | source)
XLA Modules:
  0.0 62.0 jit_solution(15903176511871043293)
XLA Ops:
  0.0 60.6 %shard_map.136 = bf16[2,32,224]{2,1,0:T(8,128)(2,1)} custom-call(s32[32]{0:T(128)} %slot_s.1, s32[4,8]{1,0:T(4,128)} %bitcast.11, s32[4]{0:T(128)} %ctx_s.1, bf16[576,128]{1,0:T(8,128)(2,1)} %bitcast.9, bf16[4,576,1024]{2,1,0:T(8,128)(2,1)} %bitcast.8, bf16[2,4,32,576]{3,2,1,0:T(8,128)(2,1)} %qry_h.1, bf16[2,4,576]{2,1,0:T(4,128)(2,1)} %stp_h.1, ...), custom_call_target="tpu_custom_call" | custom-call | flops 4000000000 | bytes 42000000 | tf_op jit(solution)/shard_map/pallas_call | solution.py:862
  60.6 1.4 %copy.16 = bf16[2,32,224]{2,1,0:T(8,128)(2,1)} copy(bf16[2,32,224]{2,1,0:T(8,128)(2,1)} %shard_map.136) | data formatting | bytes 57344

commit v4 on v3

--- a/solution.py
+++ b/solution.py
@@ -414,7 +414,7 @@
         cache_exp = jnp.exp(cache_score - top)
         cache_max.append(top)
         cache_sum.append(jnp.sum(cache_exp, axis=1, keepdims=True))
-        cache_out[i] = jnp.transpose(dot_rows(kv[i, 0:LAT, :], cache_exp.astype(bf16)))
+        cache_out[i] = dot_rows(cache_exp.astype(bf16), kv[i, 0:LAT, :])
 
     for step in range(1, dp_count):
         other = lax.rem(d + step, dp_count)
@@ -582,8 +582,8 @@
         inside = (block_lane >= 64 * xx) & (block_lane < 64 * xx + pair)
         block = jnp.where(inside, block, 0.0).astype(bf16)
         first = pl.multiple_of((zz * Y_COUNT + yy) * block_width + xx * 384, 128)
-        gacc[...] += dot_rows(wg[:, pl.ds(first, WINDOW)], block)
-        uacc[...] += dot_rows(wu[:, pl.ds(first, WINDOW)], block)
+        gacc[...] += dot_rows(block, wg[:, pl.ds(first, WINDOW)])
+        uacc[...] += dot_rows(block, wu[:, pl.ds(first, WINDOW)])
         lane = pl.multiple_of(384 * (1 - xx), 128)
         sqacc[xx] += xbuf[slot, :, :, pl.ds(lane, 128)].reshape(rows, 128).astype(f32)
 
@@ -643,11 +643,10 @@
     sq_lane = lax.broadcasted_iota(jnp.int32, (rows, 128), 1)
     sq_all = jnp.where((sq_lane == pair - 384) | (sq_lane == pair - 383), sqacc[0], 0.0)
     sq_all = sq_all + jnp.where(sq_lane < 2, sqacc[1], 0.0)
-    sq_total = jnp.sum(jnp.transpose(sq_all), axis=0, keepdims=True)
+    sq_total = jnp.sum(sq_all, axis=1, keepdims=True)
     token_scale = lax.rsqrt(sq_total / (block_width * dp_count) + norm_eps)
     gate = gacc[...] * token_scale
-    hidden_units = gate / (1.0 + jnp.exp(-gate)) * (uacc[...] * token_scale)
-    by_token = jnp.transpose(hidden_units)
+    by_token = gate / (1.0 + jnp.exp(-gate)) * (uacc[...] * token_scale)
     act[0:32] = jnp.where(c == 0, by_token[0:32], by_token[32:64]).astype(bf16)
     act[32:64] = jnp.where(c == 0, by_token[32:64], by_token[0:32]).astype(bf16)
 
@@ -822,8 +821,8 @@
         pltpu.VMEM((2, 32, w_out.shape[2]), f32),
         pltpu.VMEM(pieces, f32),
         pltpu.VMEM((16, 2, *pieces), bf16),
-        pltpu.VMEM((ff_share, 64), f32),
-        pltpu.VMEM((ff_share, 64), f32),
+        pltpu.VMEM((64, ff_share), f32),
+        pltpu.VMEM((64, ff_share), f32),
         pltpu.VMEM((2, 64, 128), f32),
         pltpu.VMEM((64, ff_share), bf16),
         pltpu.VMEM((8, 2, *pieces), bf16),

time: 62.2 us -> 62.6 us (level)
  no operation moved by 1% of the time
where the time goes in v4:
time: 62.6 us; the launch traced here: 62.3 us
  Pallas kernels  60.9 us (97%)
  local copies, waits for them, and re-layouts  1.38 us (2%)
    pallas_call x1, Pallas kernels, fused_shards(): pl.pallas_call(layer_kernel, out_shape=jax.ShapeDtypeStruct(hidden.shape,...  60.9 us
    unnamed x1, local copies, waits for them, and re-layouts  1.38 us

profile of v4, /device:TPU:0, one launch (start us, length us, event | category | flops | bytes accessed | tf_op | source)
XLA Modules:
  0.0 62.3 jit_solution(16695092299803744091)
XLA Ops:
  0.0 60.9 %shard_map.136 = bf16[2,32,224]{2,1,0:T(8,128)(2,1)} custom-call(s32[32]{0:T(128)} %slot_s.1, s32[4,8]{1,0:T(4,128)} %bitcast.11, s32[4]{0:T(128)} %ctx_s.1, bf16[576,128]{1,0:T(8,128)(2,1)} %bitcast.9, bf16[4,576,1024]{2,1,0:T(8,128)(2,1)} %bitcast.8, bf16[2,4,32,576]{3,2,1,0:T(8,128)(2,1)} %qry_h.1, bf16[2,4,576]{2,1,0:T(4,128)(2,1)} %stp_h.1, ...), custom_call_target="tpu_custom_call" | custom-call | flops 4000000000 | bytes 42000000 | tf_op jit(solution)/shard_map/pallas_call | solution.py:861
  60.9 1.4 %copy.16 = bf16[2,32,224]{2,1,0:T(8,128)(2,1)} copy(bf16[2,32,224]{2,1,0:T(8,128)(2,1)} %shard_map.136) | data formatting | bytes 57344

commit v5 on v3

--- a/solution.py
+++ b/solution.py
@@ -269,7 +269,9 @@
     core_peer = (d, x * CORES + (1 - c))
 
     def z_at(step):
-        return lax.rem(z + step, Z_COUNT)
+        low = lax.rem(z + step, 2)
+        high = lax.rem(lax.div(z, 2) + lax.div(jnp.int32(step), 2), 2)
+        return high * 2 + low
 
     def send(src, dst, send_sem, recv_sem, device):
         copy = pltpu.make_async_remote_copy(
@@ -624,8 +626,8 @@
 
     def from_corner_and_use(m, carry):
         zz = z_at(m)
+        use_block(x, 1 - y, zz)
         pass_on(take(1 - x, 1 - y, zz), 3, 12 + m, core_peer)
-        use_block(x, 1 - y, zz)
         use_block(1 - x, y, zz)
         return carry
 
@@ -633,8 +635,9 @@
         use_block(1 - x, 1 - y, z_at(m))
         return carry
 
+    lax.fori_loop(1, 3, from_z, 0)
     use_block(x, y, z)
-    lax.fori_loop(1, Z_COUNT, from_z, 0)
+    from_z(jnp.int32(3), 0)
     from_sides(jnp.int32(0))
     lax.fori_loop(1, Z_COUNT, from_sides_and_use, 0)
     lax.fori_loop(0, Z_COUNT, from_corner_and_use, 0)

time: 62.2 us -> 62.4 us (level)
  no operation moved by 1% of the time
where the time goes in v5:
time: 62.4 us; the launch traced here: 62.1 us
  Pallas kernels  60.7 us (97%)
  local copies, waits for them, and re-layouts  1.38 us (2%)
    pallas_call x1, Pallas kernels, fused_shards(): pl.pallas_call(layer_kernel, out_shape=jax.ShapeDtypeStruct(hidden.shape,...  60.7 us
    unnamed x1, local copies, waits for them, and re-layouts  1.38 us

profile of v5, /device:TPU:0, one launch (start us, length us, event | category | flops | bytes accessed | tf_op | source)
XLA Modules:
  0.0 62.1 jit_solution(13626330529817270782)
XLA Ops:
  0.0 60.7 %shard_map.136 = bf16[2,32,224]{2,1,0:T(8,128)(2,1)} custom-call(s32[32]{0:T(128)} %slot_s.1, s32[4,8]{1,0:T(4,128)} %bitcast.11, s32[4]{0:T(128)} %ctx_s.1, bf16[576,128]{1,0:T(8,128)(2,1)} %bitcast.9, bf16[4,576,1024]{2,1,0:T(8,128)(2,1)} %bitcast.8, bf16[2,4,32,576]{3,2,1,0:T(8,128)(2,1)} %qry_h.1, bf16[2,4,576]{2,1,0:T(4,128)(2,1)} %stp_h.1, ...), custom_call_target="tpu_custom_call" | custom-call | flops 4000000000 | bytes 42000000 | tf_op jit(solution)/shard_map/pallas_call | solution.py:865
  60.7 1.4 %copy.16 = bf16[2,32,224]{2,1,0:T(8,128)(2,1)} copy(bf16[2,32,224]{2,1,0:T(8,128)(2,1)} %shard_map.136) | data formatting | bytes 57344
